TPU v7x, 32 devices: a whole 2x2x4 slice. The times are simulated.
32 devices in a mesh: req: 4 (over z), seq: 2 (over core), exp: 4 (over y, x).
Axes of the slice: x: 2, y: 2, z: 4, core: 2. Of those that a mesh axis runs over, the one named last changes fastest.
Arguments:
- residual: bfloat16 [64, 7168], P(('req', 'seq', 'exp')), may hold values from -6 to 6
- queries: bfloat16 [4, 16, 128, 576], P('req', None, 'exp'), may hold values from -60 to 60
- latent_cache: bfloat16 [4, 384, 576], P('req', 'seq'), may hold values from -20 to 20
- blocks: int32 [4, 2, 2], P('req', 'seq'), may hold values from 0 to 2, as said below
- lengths: int32 [4], P('req'), may hold values from 208 to 384, as said below
- value_up: bfloat16 [128, 512, 128], P('exp'), may hold values from -0.25 to 0.25
- out_proj: bfloat16 [16384, 7168], P('exp', ('req', 'seq')), may hold values from -0.046875 to 0.046875
- norm_gain: bfloat16 [7168], replicated, may hold values from 0.099609375 to 1.8984375
- router: bfloat16 [7168, 4], replicated, may hold values from -0.0625 to 0.0625
- expert_ids: int32 [64, 2], P(('req', 'seq', 'exp')), may hold values from 0 to 3, all different within a row; in each aligned block of 2 rows (0 to 1, 2 to 3, ...) at most 2 rows name the same one
- w_gate: bfloat16 [4, 7168, 2048], P('req', None, ('seq', 'exp')), may hold values from -0.0625 to 0.0625
- w_up: bfloat16 [4, 7168, 2048], P('req', None, ('seq', 'exp')), may hold values from -0.0625 to 0.0625
- w_down: bfloat16 [4, 2048, 7168], P('req', ('seq', 'exp')), may hold values from -0.125 to 0.125
Outputs:
- layer_out: bfloat16 [64, 7168], P(('req', 'seq', 'exp'))
Inputs may be any that keep to these rules, and one draw needn't show every extreme that they name: `blocks`: each request and shard lists 2 different block numbers of that shard. `lengths`: some request has exactly 384, some exactly 208. `expert_ids`: each row names 2 different experts; among the rows of one device (aligned blocks of 2 rows) no expert is named more than 2 times, a bound that some block reaches.
All inputs are finite; a program needn't handle non-finite values.
Results may differ from a plain program's by a relative error of at most 0.019.
Values may be sent and summed in bfloat16 or wider, within the bound.
A program may use at most 128 MiB of HBM per device.

v0:
```python
import jax
import jax.numpy as jnp
from jax import lax
from jax.sharding import PartitionSpec as P

DL = 512
DR = 64
DV = 128
BLOCK = 64


def merge_parts(former, latter):
    row_max = jnp.maximum(former[0], latter[0])
    left_scale = jnp.exp(former[0] - row_max)
    right_scale = jnp.exp(latter[0] - row_max)
    return (
        row_max,
        left_scale * former[1] + right_scale * latter[1],
        left_scale[..., None] * former[2] + right_scale[..., None] * latter[2],
    )


def pick_rows(block_rows, picks):
    return block_rows[picks]


def shard_softmax(queries, picked, usable):
    scores = jnp.einsum("bqhk,bjk->bqhj", queries, picked, preferred_element_type=jnp.float32) * (
        DV + DR
    ) ** (-0.5)
    row_max = jnp.max(jnp.where(usable, scores, -1e30), axis=-1)
    weights = jnp.where(usable, jnp.exp(scores - row_max[..., None]), 0.0).astype(jnp.bfloat16)
    row_sum = jnp.sum(weights.astype(jnp.float32), -1)
    weighted = jnp.einsum(
        "bqhj,bjd->bqhd", weights, picked[..., :DL], preferred_element_type=jnp.float32
    )
    return (row_max, row_sum, weighted)


def expert_rows(arrived, w_gate, w_up, w_down):
    model_width = w_gate.shape[1]
    flat_rows = arrived.reshape(-1, model_width)
    gate_act = jnp.dot(flat_rows, w_gate[0], preferred_element_type=jnp.float32)
    up_act = jnp.dot(flat_rows, w_up[0], preferred_element_type=jnp.float32)
    activated = (jax.nn.silu(gate_act) * up_act).astype(jnp.bfloat16)
    partial_value = jnp.dot(activated, w_down[0], preferred_element_type=jnp.float32).astype(
        jnp.bfloat16
    )
    return partial_value.reshape(arrived.shape)


def per_device(
    residual,
    queries,
    latent_cache,
    blocks,
    lengths,
    value_up,
    out_proj,
    norm_gain,
    router,
    expert_ids,
    w_gate,
    w_up,
    w_down,
):
    local_reqs, drafts, head_count, qk_width = queries.shape
    shard_len = latent_cache.shape[1]
    picks_count = blocks.shape[2]
    seq_index = lax.axis_index("seq")
    block_view = latent_cache.reshape(local_reqs, shard_len // BLOCK, BLOCK, qk_width)
    picked = jax.vmap(pick_rows)(block_view, blocks[:, 0]).reshape(
        local_reqs, picks_count * BLOCK, qk_width
    )
    positions = (
        seq_index * shard_len + blocks[:, 0, :, None] * BLOCK + jnp.arange(BLOCK, dtype=jnp.int32)
    )
    positions = positions.reshape(local_reqs, picks_count * BLOCK)
    limits = lengths[:, None] - (drafts - 1) + jnp.arange(drafts, dtype=jnp.int32)[None, :]
    usable = positions[:, None, None, :] < limits[:, :, None, None]
    usable_mark = usable[:, :, 0, :].astype(jnp.bfloat16)
    all_keys, all_marks = (
        lax.all_gather(picked[None], "seq", axis=0, tiled=True),
        lax.all_gather(usable_mark[None], "seq", axis=0, tiled=True),
    )
    combined = None
    for shard in range(lax.axis_size("seq")):
        shard_usable = (all_marks[shard] > 0)[:, :, None, :]
        partial_value = shard_softmax(queries, all_keys[shard], shard_usable)
        combined = partial_value if combined is None else merge_parts(combined, partial_value)
    latent = (combined[2] / combined[1][..., None]).astype(jnp.bfloat16)
    head_values = jnp.einsum(
        "bqhd,hdv->bqhv", latent, value_up, preferred_element_type=jnp.float32
    ).astype(jnp.bfloat16)
    flat_values = head_values.reshape(local_reqs * drafts, head_count * DV)
    col_terms = jnp.dot(
        lax.all_gather(flat_values, "req", axis=0, tiled=True),
        out_proj,
        preferred_element_type=jnp.float32,
    )
    token_terms = lax.all_to_all(
        col_terms[None].astype(jnp.bfloat16),
        ("req", "seq", "exp"),
        split_axis=1,
        concat_axis=0,
        tiled=True,
    ).astype(jnp.float32)
    exp_count = lax.axis_size("exp")
    col_blocks = token_terms.shape[0] // exp_count
    rows_here = token_terms.shape[1]
    col_sums = jnp.sum(
        token_terms.reshape(col_blocks, exp_count, rows_here, token_terms.shape[2]), 1
    )
    attended = jnp.transpose(col_sums, (1, 0, 2)).reshape(rows_here, -1).astype(jnp.bfloat16)
    hidden_sum = (residual.astype(jnp.float32) + attended.astype(jnp.float32)).astype(jnp.bfloat16)
    hidden32 = hidden_sum.astype(jnp.float32)
    normed = (
        hidden32
        * lax.rsqrt(jnp.mean(hidden32 * hidden32, -1, keepdims=True) + 1e-06)
        * norm_gain.astype(jnp.float32)
    ).astype(jnp.bfloat16)
    gate_probs = jax.nn.sigmoid(jnp.dot(normed, router, preferred_element_type=jnp.float32))
    expert_count = router.shape[1]
    top_count = expert_ids.shape[1]
    one_hot = (expert_ids[:, :, None] == jnp.arange(expert_count, dtype=jnp.int32)).astype(
        jnp.int32
    )
    pair_hot = one_hot.reshape(rows_here * top_count, expert_count)
    slot_index = jnp.sum((jnp.cumsum(pair_hot, 0) - pair_hot) * pair_hot, -1)
    slot_hot = (slot_index[:, None] == jnp.arange(rows_here, dtype=jnp.int32)).astype(jnp.int32)
    placement = (pair_hot[:, :, None] * slot_hot[:, None, :]).reshape(
        rows_here, top_count, expert_count * rows_here
    )
    chosen = jnp.sum(one_hot.astype(jnp.float32) * gate_probs[:, None, :], -1)
    gate_weights = chosen / jnp.sum(chosen, -1, keepdims=True) * 2.5
    dispatch = jnp.sum(placement, 1).astype(jnp.bfloat16)
    outgoing = jnp.dot(dispatch.T, normed, preferred_element_type=jnp.float32).astype(jnp.bfloat16)
    outgoing = outgoing.reshape(expert_count, rows_here, outgoing.shape[1])
    combine = jnp.sum(gate_weights[:, :, None] * placement.astype(jnp.float32), 1)
    copies = lax.axis_size("seq") * exp_count
    fanned = jnp.broadcast_to(outgoing[:, None], (expert_count, copies) + outgoing.shape[1:])
    fanned = fanned.reshape((expert_count * copies,) + outgoing.shape[1:])
    returned = lax.all_to_all(
        expert_rows(
            lax.all_to_all(fanned, ("req", "seq", "exp"), split_axis=0, concat_axis=0, tiled=True),
            w_gate,
            w_up,
            w_down,
        ),
        ("req", "seq", "exp"),
        split_axis=0,
        concat_axis=0,
        tiled=True,
    )
    returned = returned.reshape((expert_count, copies) + outgoing.shape[1:]).astype(jnp.float32)
    expert_out = jnp.sum(returned, 1).astype(jnp.bfloat16)
    slot_rows = expert_out.reshape(expert_count * rows_here, expert_out.shape[2]).astype(
        jnp.float32
    )
    routed = jnp.dot(combine, slot_rows, precision=lax.Precision.HIGHEST)
    return (hidden32 + routed).astype(jnp.bfloat16)


def solution(mesh):
    in_specs = (
        P(("req", "seq", "exp"), None),
        P("req", None, "exp", None),
        P("req", "seq", None),
        P("req", "seq", None),
        P("req"),
        P("exp", None, None),
        P("exp", ("req", "seq")),
        P(),
        P(),
        P(("req", "seq", "exp"), None),
        P("req", None, ("seq", "exp")),
        P("req", None, ("seq", "exp")),
        P("req", ("seq", "exp"), None),
    )
    out_specs = P(("req", "seq", "exp"), None)
    return jax.shard_map(
        per_device, mesh=mesh, in_specs=in_specs, out_specs=out_specs, check_vma=False
    )
```

profile of v0, /device:TPU:0, one launch (start us, length us, event | category | flops | bytes accessed | tf_op | source)
XLA Modules:
  0.0 118.2 jit_solution(12119683160606463173)
XLA Ops:
  0.7 0.7 compare_select_fusion
  1.4 0.7 add_bitcast_fusion
  2.1 0.1 add.105
  2.2 0.1 copy.62
  2.3 0.1 pad_bitcast_fusion
  2.4 0.2 or_reduce_fusion
  2.6 0.1 add.107
  2.7 0.1 compare_convert_fusion
  2.7 1.9 %all_gather.9 = bf16[2,1,16,128]{3,2,1,0:T(8,128)(2,1)S(1)} all-gather(bf16[1,1,16,128]{3,2,1,0:T(8,128)(2,1)S(1)} %compare_convert_fusion), channel_id=1, replica_groups=mesh['req'=4,'seq'=2,'exp'=4] {'seq'}, dimensions={0}, use_global_device_ids=true | all-gather | bytes 12288 | tf_op jit(solution)/shard_map/all_gather | solution.py:84
  4.7 1.5 %gather_fusion = bf16[2,64,576]{2,1,0:T(8,128)(2,1)S(1)} fusion(bf16[1,3,64,576]{3,2,1,0:T(8,128)(2,1)} %bitcast.110, s32[2]{0:T(128)S(1)} %or_reduce_fusion), kind=kCustom, calls=%fused_computation | custom fusion | bytes 294928 | tf_op jit(solution)/shard_map/vmap()/gather | solution.py:24
  6.2 0.1 copy.47
  6.3 2.0 %all_gather.10 = bf16[2,1,128,576]{2,3,1,0:T(8,128)(2,1)S(1)} all-gather(bf16[1,1,128,576]{2,3,1,0:T(8,128)(2,1)S(1)} %copy.47), channel_id=1, replica_groups=mesh['req'=4,'seq'=2,'exp'=4] {'seq'}, dimensions={0}, use_global_device_ids=true | all-gather | bytes 442368 | tf_op jit(solution)/shard_map/all_gather | solution.py:83
  8.4 0.4 select_reduce_fusion
  8.8 0.4 select_reduce_fusion.1
  9.2 0.4 convert_reduce_fusion
  9.7 0.1 copy.54
  9.9 0.3 convolution_multiply_fusion
  10.2 3.0 %fusion.13 = bf16[1,16,32,128]{3,1,2,0:T(8,128)(2,1)S(1)} fusion(bf16[32,512,128]{2,1,0:T(8,128)(2,1)} %param.18, f32[16,32,512]{2,0,1:T(8,128)S(1)} %convolution_multiply_fusion, f32[16,32]{0,1:T(8,128)S(1)} %copy.54, f32[16,32]{0,1:T(8,128)S(1)} %copy.48, bf16[1,128,576]{1,2,0:T(8,128)(2,1)S(1)} %get-tuple-element.16, ...), kind=kOutput, calls=%fused_computation.22 | convolution fusion | flops 135331840 | bytes 5668864 | tf_op jit(solution)/shard_map/bqhd,hdv->bqhv/dot_general | solution.py:92
  13.3 17.6 %all_gather.11 = bf16[64,4096]{1,0:T(8,128)(2,1)S(1)} all-gather(bf16[16,4096]{1,0:T(8,128)(2,1)S(1)} %bitcast.107), channel_id=1, replica_groups=mesh['req'=4,'seq'=2,'exp'=4] {'req'}, dimensions={0}, use_global_device_ids=true | all-gather | bytes 655360 | tf_op jit(solution)/shard_map/all_gather | solution.py:97
  30.9 4.4 %fusion.14 = bf16[1,64,896]{2,1,0:T(8,128)(2,1)S(1)} fusion(bf16[64,4096]{1,0:T(8,128)(2,1)S(1)} %all_gather.11, bf16[4096,896]{1,0:T(8,128)(2,1)} %param.19), kind=kOutput, calls=%fused_computation.23 | convolution fusion | flops 469819392 | bytes 7979008 | tf_op jit(solution)/shard_map/dot_general | solution.py:96
  35.3 0.2 copy.72
  35.5 0.5 broadcast.257
  36.0 1.3 %reduce.15 = bf16[64,896]{1,0:T(8,128)(2,1)S(1)} reduce(bf16[64,1,896]{2,1,0:T(2,128)(2,1)S(1)} %bitcast.105, bf16[]{:T(256)} %broadcast.257), dimensions={1}, to_apply=%bitcast.103.reduce_sub_computation | reduce | bytes 229378
  37.3 0.7 reshape.413
  38.0 6.0 %all-to-all-start = ((bf16[32,2,896]{2,1,0:T(2,128)(2,1)}), bf16[32,2,896]{2,1,0:T(2,128)(2,1)S(1)}, u32[]{:S(2)}, u32[]{:S(2)}) async-start(bf16[32,2,896]{2,1,0:T(2,128)(2,1)} %reshape.413), calls=%async_computation | async-start | bytes 229376 | tf_op jit(solution)/shard_map/all_to_all | solution.py:101
  44.0 0.1 eq.46
  44.2 0.2 select_reduce_fusion.2
  44.5 0.1 mul.156
  44.7 7.5 %all-to-all-done = bf16[32,2,896]{2,1,0:T(2,128)(2,1)S(1)} async-done(((bf16[32,2,896]{2,1,0:T(2,128)(2,1)}), bf16[32,2,896]{2,1,0:T(2,128)(2,1)S(1)}, u32[]{:S(2)}, u32[]{:S(2)}) %all-to-all-start) | async-done | bytes 114720 | tf_op jit(solution)/shard_map/all_to_all | solution.py:101
  52.2 0.1 reshape.414
  52.3 0.6 bitcast_reduce_fusion.1
  52.9 0.1 reduce.10
  53.1 0.2 fusion.42
  53.3 0.2 convolution_convert_fusion.1
  53.6 0.5 broadcast_in_dim.64
  54.1 25.6 %all_to_all.19 = bf16[32,2,7168]{2,1,0:T(2,128)(2,1)S(1)} all-to-all(bf16[32,2,7168]{2,1,0:T(2,128)(2,1)S(1)} %bitcast.104), channel_id=1, replica_groups=mesh['req'=4,'seq'=2,'exp'=4] {'req','seq','exp'}, dimensions={0} | all-to-all | bytes 1835008 | tf_op jit(solution)/shard_map/all_to_all | solution.py:145
  79.7 0.3 reshape.393
  80.1 2.8 %fusion.4 = f32[64,256]{1,0:T(8,128)S(1)} fusion(bf16[64,7168]{1,0:T(8,128)(2,1)S(1)} %reshape.393, bf16[1,7168,256]{2,1,0:T(8,128)(2,1)} %param.23), kind=kOutput, calls=%fused_computation.8 | convolution fusion | flops 234881024 | bytes 4653056 | tf_op jit(solution)/shard_map/dot_general | solution.py:43
  82.8 5.5 %convolution_convert_fusion = bf16[64,7168]{1,0:T(8,128)(2,1)S(1)} fusion(bf16[1,256,7168]{2,1,0:T(8,128)(2,1)} %param.25, bf16[64,7168]{1,0:T(8,128)(2,1)S(1)} %reshape.393, bf16[1,7168,256]{2,1,0:T(8,128)(2,1)} %param.24, f32[64,256]{1,0:T(8,128)S(1)} %fusion.4), kind=kOutput, calls=%fused_computation.1 | convolution fusion | flops 470319104 | bytes 9240576 | tf_op jit(solution)/shard_map/dot_general | solution.py:46
  88.3 1.3 %reshape.394 = bf16[32,2,7168]{2,1,0:T(2,128)(2,1)} reshape(bf16[64,7168]{1,0:T(8,128)(2,1)S(1)} %convolution_convert_fusion) | data formatting | bytes 1835008 | tf_op jit(solution)/shard_map/reshape | solution.py:49
  89.6 3.1 %all-to-all-start.2 = ((bf16[32,2,7168]{2,1,0:T(2,128)(2,1)}), bf16[32,2,7168]{2,1,0:T(2,128)(2,1)S(1)}, u32[]{:S(2)}, u32[]{:S(2)}) async-start(bf16[32,2,7168]{2,1,0:T(2,128)(2,1)} %reshape.394), calls=%async_computation.2 | async-start | bytes 1835008 | tf_op jit(solution)/shard_map/all_to_all | solution.py:143
  92.6 0.2 fusion.23
  92.9 0.2 fusion.51
  93.1 0.1 divide_multiply_fusion
  93.1 0.1 multiply_reduce_fusion
  93.2 23.3 %all-to-all-done.2 = bf16[32,2,7168]{2,1,0:T(2,128)(2,1)S(1)} async-done(((bf16[32,2,7168]{2,1,0:T(2,128)(2,1)}), bf16[32,2,7168]{2,1,0:T(2,128)(2,1)S(1)}, u32[]{:S(2)}, u32[]{:S(2)}) %all-to-all-start.2) | async-done | bytes 917536 | tf_op jit(solution)/shard_map/all_to_all | solution.py:143
  116.5 0.8 bitcast_reduce_fusion
  117.4 0.9 fusion
  (32 shorter events, 0.9 us)
Async XLA Ops:
  0.0 8.4 %copy-start = (bf16[1,16,32,576]{3,2,1,0:T(8,128)(2,1)S(1)}, bf16[1,16,32,576]{3,2,1,0:T(8,128)(2,1)}, u32[]{:S(2)}) copy-start(bf16[1,16,32,576]{3,2,1,0:T(8,128)(2,1)} %param.14) | copy-start | bytes 1769476
  30.9 13.1 %copy-start.3 = (s32[2,2]{1,0:T(2,128)S(1)}, s32[2,2]{1,0:T(2,128)}, u32[]{:S(2)}) copy-start(s32[2,2]{1,0:T(2,128)} %param.22) | copy-start | bytes 52
  30.9 13.7 %copy-start.2 = (bf16[7168]{0:T(1024)(128)(2,1)S(1)}, bf16[7168]{0:T(1024)(128)(2,1)}, u32[]{:S(2)}) copy-start(bf16[7168]{0:T(1024)(128)(2,1)} %param.20) | copy-start | bytes 43012
  30.9 22.2 %copy-start.1 = (bf16[2,7168]{1,0:T(2,128)(2,1)S(1)}, bf16[2,7168]{1,0:T(2,128)(2,1)}, u32[]{:S(2)}) copy-start(bf16[2,7168]{1,0:T(2,128)(2,1)} %param.13) | copy-start | bytes 86020
  38.0 14.2 %all-to-all-start = ((bf16[32,2,896]{2,1,0:T(2,128)(2,1)}), bf16[32,2,896]{2,1,0:T(2,128)(2,1)S(1)}, u32[]{:S(2)}, u32[]{:S(2)}) async-start(bf16[32,2,896]{2,1,0:T(2,128)(2,1)} %reshape.413), calls=%async_computation | async-start | bytes 229376 | tf_op jit(solution)/shard_map/all_to_all | solution.py:101
  88.3 4.4 %copy-start.4 = (bf16[7168,4]{0,1:T(4,128)(2,1)S(1)}, bf16[7168,4]{0,1:T(4,128)(2,1)}, u32[]{:S(2)}) copy-start(bf16[7168,4]{0,1:T(4,128)(2,1)} %param.21) | copy-start | bytes 172036
  89.6 27.0 %all-to-all-start.2 = ((bf16[32,2,7168]{2,1,0:T(2,128)(2,1)}), bf16[32,2,7168]{2,1,0:T(2,128)(2,1)S(1)}, u32[]{:S(2)}, u32[]{:S(2)}) async-start(bf16[32,2,7168]{2,1,0:T(2,128)(2,1)} %reshape.394), calls=%async_computation.2 | async-start | bytes 1835008 | tf_op jit(solution)/shard_map/all_to_all | solution.py:143
where the time goes:
time: 119 us; the launch traced here: 118 us
  blocking collectives  47.1 us (40%)
  waiting for transfers between devices  30.8 us (26%)
  matrix products  18.1 us (15%)
  starting transfers between devices  9.07 us (8%)
  local copies, waits for them, and re-layouts  6.93 us (6%)
  other arithmetic  5.23 us (4%)
    all_to_all x1, blocking collectives, per_device(): lax.all_to_all(fanned, ('req', 'seq', 'exp'), split_axis=0, concat_axis=0...  25.6 us
    all_to_all x1, waiting for transfers between devices, per_device(): lax.all_to_all(expert_rows(lax.all_to_all(fanned, ('req', 'seq', 'exp'),...  23.3 us
    all_gather x1, blocking collectives, per_device(): lax.all_gather(flat_values, 'req', axis=0, tiled=True)  17.6 us
    all_to_all x1, waiting for transfers between devices, per_device(): lax.all_to_all(col_terms[None].astype(jnp.bfloat16), ('req', 'seq', 'exp'...  7.51 us
    all_to_all x1, starting transfers between devices, per_device(): lax.all_to_all(col_terms[None].astype(jnp.bfloat16), ('req', 'seq', 'exp'...  6.01 us
    dot_general x1, matrix products, expert_rows(): jnp.dot(activated, w_down[0], preferred_element_type=jnp.float32)  5.45 us
    dot_general x1, matrix products, per_device(): jnp.dot(lax.all_gather(flat_values, 'req', axis=0, tiled=True), out_proj,...  4.36 us
    all_to_all x1, starting transfers between devices, per_device(): lax.all_to_all(expert_rows(lax.all_to_all(fanned, ('req', 'seq', 'exp'),...  3.06 us
  transfers between devices with their start and end apart: 2, of which 2 were waited for; matrix products, arithmetic and copies ran while one was open for 1% of the time, Pallas kernels for 0%

commit v1 on v0

--- a/solution.py
+++ b/solution.py
@@ -1,6 +1,10 @@
+import functools
+
 import jax
 import jax.numpy as jnp
 from jax import lax
+from jax.experimental import pallas as pl
+from jax.experimental.pallas import tpu as pltpu
 from jax.sharding import PartitionSpec as P
 
 DL = 512
@@ -161,6 +165,496 @@
     return (hidden32 + routed).astype(jnp.bfloat16)
 
 
+MESH = pl.DeviceIdType.MESH
+
+
+def fused_kernel(
+    dims,
+    residual_ref,
+    queries_hbm,
+    cache_ref,
+    blocks_ref,
+    lengths_ref,
+    value_up_hbm,
+    out_proj_hbm,
+    gain_ref,
+    router_hbm,
+    ids_ref,
+    w_gate_hbm,
+    w_up_hbm,
+    w_down_hbm,
+    out_ref,
+    q_v,
+    vu_v,
+    op_v,
+    rt_v,
+    wg_v,
+    wu_v,
+    wd_v,
+    keys_rx,
+    marks,
+    res_tx,
+    res_rx,
+    lat,
+    hv,
+    acc,
+    part_tx,
+    part_rx,
+    res_sum,
+    xs,
+    ys,
+    y_tx,
+    y_rx,
+    z_sum,
+    z_tx,
+    z_rx,
+    f_tx,
+    f_rx,
+    load_sem,
+    key_sem,
+    mark_sem,
+    res_ssem,
+    res_rsem,
+    hz_ssem,
+    hz_rsem,
+    hs_ssem,
+    hs_rsem,
+    ps_ssem,
+    ps_rsem,
+    az_ssem,
+    az_rsem,
+    ae_ssem,
+    ae_rsem,
+    as_ssem,
+    as_rsem,
+    ys_ssem,
+    ys_rsem,
+    ye_ssem,
+    ye_rsem,
+    yz_ssem,
+    yz_rsem,
+):
+    R, S, E = dims
+    f32, b16 = jnp.float32, jnp.bfloat16
+    r, s, e = lax.axis_index("req"), lax.axis_index("seq"), lax.axis_index("exp")
+    other = 1 - s
+    sibling = (r, other, e)
+    drafts, half_heads, _ = q_v.shape
+    keys_len = cache_ref.shape[0]
+    width = op_v.shape[1]
+    chunks = R * S
+    nt = residual_ref.shape[0]
+    devices = R * S * E
+    mine = r * S + s
+    at_home = (e == r).astype(jnp.int32)
+
+    head_from = pl.multiple_of(s * half_heads, half_heads)
+    loads = [
+        pltpu.make_async_copy(queries_hbm.at[:, pl.ds(head_from, half_heads), :], q_v, load_sem.at[0]),
+        pltpu.make_async_copy(value_up_hbm.at[pl.ds(head_from, half_heads)], vu_v, load_sem.at[1]),
+        pltpu.make_async_copy(out_proj_hbm, op_v, load_sem.at[2]),
+        pltpu.make_async_copy(router_hbm, rt_v, load_sem.at[3]),
+        pltpu.make_async_copy(w_gate_hbm, wg_v, load_sem.at[4]),
+        pltpu.make_async_copy(w_up_hbm, wu_v, load_sem.at[5]),
+        pltpu.make_async_copy(w_down_hbm, wd_v, load_sem.at[6]),
+    ]
+    for load in loads:
+        load.start()
+
+    def z_peer(d):
+        return (lax.rem(r + d, R), s, e)
+
+    def e_peer(d):
+        return (r, s, lax.rem(e + d, E))
+
+    barrier = pltpu.get_barrier_semaphore()
+    for peer in [sibling] + [z_peer(d) for d in range(1, R)] + [e_peer(d) for d in range(1, E)]:
+        pl.semaphore_signal(barrier, inc=1, device_id=peer, device_id_type=MESH)
+    for ss in range(S):
+        for ee in range(E):
+
+            @pl.when(jnp.logical_not((e == r) & (s == ss) & (e == ee)))
+            def _():
+                pl.semaphore_signal(barrier, inc=1, device_id=(e, ss, ee), device_id_type=MESH)
+
+    block_of = lax.broadcasted_iota(jnp.int32, marks.shape[1:], 1) // BLOCK
+    hit = block_of == blocks_ref[0]
+    for i in range(1, blocks_ref.shape[0]):
+        hit = hit | (block_of == blocks_ref[i])
+    marks[0] = hit.astype(f32)
+    lane = lax.broadcasted_iota(jnp.int32, (1, 128), 1)
+    for t in range(nt):
+        hot = lane == ids_ref[t, 0]
+        for k in range(1, ids_ref.shape[1]):
+            hot = hot | (lane == ids_ref[t, k])
+        for c in range(chunks):
+            res_tx[c, t : t + 1, width:] = hot.astype(f32)
+    for c in range(chunks):
+        res_tx[c, :, :width] = residual_ref[:, c * width : (c + 1) * width].astype(f32)
+
+    pl.semaphore_wait(barrier, 1 + (R - 1) + (E - 1) + S * E - at_home)
+
+    def remote(src, dst, ssem, rsem, peer):
+        return pltpu.make_async_remote_copy(
+            src_ref=src, dst_ref=dst, send_sem=ssem, recv_sem=rsem, device_id=peer, device_id_type=MESH
+        )
+
+    sent = []
+    key_copy = remote(cache_ref, keys_rx, key_sem.at[0], key_sem.at[1], sibling)
+    mark_copy = remote(marks.at[0], marks.at[1], mark_sem.at[0], mark_sem.at[1], sibling)
+    key_copy.start()
+    mark_copy.start()
+    sent += [key_copy, mark_copy]
+    slot = s * E + e
+    for c in range(chunks):
+        to = (c // S, c % S, r)
+        here = (r == c // S) & (s == c % S) & (e == r)
+
+        @pl.when(jnp.logical_not(here))
+        def _():
+            remote(res_tx.at[c], res_rx.at[slot], res_ssem.at[c], res_rsem.at[slot], to).start()
+
+        @pl.when(here)
+        def _():
+            pltpu.make_async_copy(res_tx.at[c], res_rx.at[slot], res_rsem.at[slot]).start()
+
+    loads[0].wait()
+    q2 = q_v[...].reshape(drafts * half_heads, q_v.shape[2])
+    rows = drafts * half_heads
+    limit = lengths_ref[0] - (drafts - 1) + lax.broadcasted_iota(jnp.int32, (rows, 1), 0) // half_heads
+
+    def scores_of(keys, mark, shard):
+        sc = lax.dot_general(q2, keys, (((1,), (1,)), ((), ())), preferred_element_type=f32)
+        pos = shard * keys_len + lax.broadcasted_iota(jnp.int32, (rows, keys_len), 1)
+        usable = (pos < limit) & (mark > 0)
+        return jnp.where(usable, sc * (DV + DR) ** (-0.5), -1e30), usable
+
+    near, near_ok = scores_of(cache_ref[...], marks[0, :1, :keys_len], s)
+    key_copy.wait_recv()
+    mark_copy.wait_recv()
+    far, far_ok = scores_of(keys_rx[...], marks[1, :1, :keys_len], other)
+    top = jnp.maximum(jnp.max(near, -1, keepdims=True), jnp.max(far, -1, keepdims=True))
+    near_p = jnp.where(near_ok, jnp.exp(near - top), 0.0).astype(b16)
+    far_p = jnp.where(far_ok, jnp.exp(far - top), 0.0).astype(b16)
+    total = jnp.sum(near_p.astype(f32), -1, keepdims=True) + jnp.sum(far_p.astype(f32), -1, keepdims=True)
+    weighted = jnp.dot(near_p, cache_ref[:, :DL], preferred_element_type=f32)
+    weighted += jnp.dot(far_p, keys_rx[:, :DL], preferred_element_type=f32)
+    latent = weighted / total
+    for k in range(lat.shape[0]):
+        lat[k] = latent[:, k * 128 : (k + 1) * 128]
+
+    loads[1].wait()
+    for h in range(half_heads):
+        one = [lat[k, pl.ds(h, drafts, stride=half_heads), :] for k in range(lat.shape[0])]
+        one = jnp.concatenate(one, axis=1).astype(b16)
+        hv[s, r, :, h * DV : (h + 1) * DV] = jnp.dot(one, vu_v[h], preferred_element_type=f32).astype(b16)
+
+    hz = [
+        remote(hv.at[s, r], hv.at[s, r], hz_ssem.at[d - 1], hz_rsem.at[d - 1], z_peer(d)) for d in range(1, R)
+    ]
+    for copy in hz:
+        copy.start()
+    hs = []
+    for d in range(R):
+        if d:
+            hz[d - 1].wait_recv()
+        origin = lax.rem(r + R - d, R)
+        copy = remote(hv.at[s, origin], hv.at[s, origin], hs_ssem.at[d], hs_rsem.at[d], sibling)
+        copy.start()
+        hs.append(copy)
+    sent += hz + hs
+
+    loads[2].wait()
+    half = half_heads * DV
+
+    def out_part(side):
+        head_rows = hv[side].reshape(R * drafts, half)
+        return jnp.dot(head_rows, op_v[pl.ds(pl.multiple_of(side * half, half), half), :], preferred_element_type=f32)
+
+    acc[...] = out_part(s).reshape(acc.shape)
+    for j in range(S * E):
+        pltpu.make_async_copy(res_rx.at[j], res_rx.at[j], res_rsem.at[j]).wait()
+        res_sum[j * nt : (j + 1) * nt, :] = res_rx[j]
+    for copy in hs:
+        copy.wait_recv()
+    acc[...] += out_part(other).reshape(acc.shape)
+    part_tx[...] = acc[...].astype(b16)
+    ps = [
+        remote(part_tx.at[lax.rem(e + d, E)], part_rx.at[d - 1], ps_ssem.at[d - 1], ps_rsem.at[d - 1], e_peer(d))
+        for d in range(1, E)
+    ]
+    for copy in ps:
+        copy.start()
+    attended = acc[e]
+    for d in range(1, E):
+        ps[d - 1].wait_recv()
+        attended += part_rx[d - 1].astype(f32)
+    sent += ps
+    hidden = res_sum[:, :width] + attended.astype(b16).astype(f32)
+    xs[mine, e, :, :width] = hidden.astype(b16)
+    xs[mine, e, :, width:] = res_sum[:, width:].astype(b16)
+
+    az = [
+        remote(xs.at[mine, e], xs.at[mine, e], az_ssem.at[d - 1], az_rsem.at[d - 1], z_peer(d)) for d in range(1, R)
+    ]
+    for copy in az:
+        copy.start()
+    ae = []
+    for dz in range(R):
+        if dz:
+            az[dz - 1].wait_recv()
+        chunk = lax.rem(r + R - dz, R) * S + s
+        row = [
+            remote(xs.at[chunk, e], xs.at[chunk, e], ae_ssem.at[dz, d - 1], ae_rsem.at[dz, d - 1], e_peer(d))
+            for d in range(1, E)
+        ]
+        for copy in row:
+            copy.start()
+        ae.append(row)
+    for load in loads[3:6]:
+        load.wait()
+
+    tokens = E * xs.shape[2]
+
+    def expert_part(state, chunk):
+        squares, gate, up, logits = state
+        hid = xs[chunk].reshape(tokens, xs.shape[3])[:, :width].astype(f32)
+        cols = pl.ds(pl.multiple_of(chunk * width, width), width)
+        scaled = (hid * gain_ref[:, cols].astype(f32)).astype(b16)
+        return (
+            squares + jnp.sum(hid * hid, -1, keepdims=True),
+            gate + jnp.dot(scaled, wg_v[cols, :], preferred_element_type=f32),
+            up + jnp.dot(scaled, wu_v[cols, :], preferred_element_type=f32),
+            logits + lax.dot_general(scaled, rt_v[:, cols], (((1,), (1,)), ((), ())), preferred_element_type=f32),
+        )
+
+    state = (
+        jnp.zeros((tokens, 1), f32),
+        jnp.zeros((tokens, wg_v.shape[1]), f32),
+        jnp.zeros((tokens, wg_v.shape[1]), f32),
+        jnp.zeros((tokens, rt_v.shape[0]), f32),
+    )
+    across = []
+    for dz in range(R):
+        for copy in ae[dz]:
+            copy.wait_recv()
+        chunk = lax.rem(r + R - dz, R) * S + s
+        copy = remote(xs.at[chunk], xs.at[chunk], as_ssem.at[dz], as_rsem.at[dz], sibling)
+        copy.start()
+        across.append(copy)
+        state = expert_part(state, chunk)
+    for dz in range(R):
+        across[dz].wait_recv()
+        state = expert_part(state, lax.rem(r + R - dz, R) * S + other)
+    sent += az + [copy for row in ae for copy in row] + across
+    squares, gate, up, logits = state
+    scale = lax.rsqrt(squares / (chunks * width) + 1e-06)
+    experts = rt_v.shape[0]
+    hots = xs[mine].reshape(tokens, xs.shape[3])[:, width : width + experts].astype(f32)
+    chosen = hots * jax.nn.sigmoid(logits * scale)
+    this_expert = lax.broadcasted_iota(jnp.int32, (1, experts), 1) == r
+    weight = jnp.sum(jnp.where(this_expert, chosen, 0.0), -1, keepdims=True)
+    weight = weight / jnp.sum(chosen, -1, keepdims=True) * 2.5
+    activated = (jax.nn.silu(gate * scale) * (up * scale) * weight).astype(b16)
+
+    to_row = lax.broadcasted_iota(jnp.int32, (tokens, tokens), 0)
+    from_row = lax.broadcasted_iota(jnp.int32, (tokens, tokens), 1)
+    owner = to_row % devices
+    wanted = ((owner % R) * (S * E) + owner // R) * nt + to_row // devices
+    ordered = jnp.dot((wanted == from_row).astype(b16), activated, preferred_element_type=f32).astype(b16)
+    loads[6].wait()
+    per_owner = nt * chunks
+    planes = width // 128
+    for c in range(chunks):
+        down = jnp.dot(ordered, wd_v[:, c * width : (c + 1) * width], preferred_element_type=f32)
+        for t in range(nt):
+            part = down[t * devices : (t + 1) * devices]
+            for k in range(planes):
+                ys[k, pl.ds(c * nt + t, devices, stride=per_owner), :] = part[:, k * 128 : (k + 1) * 128]
+
+    span = R * per_owner
+    order = list(range(1, E)) + [0]
+    yc = {}
+
+    def summed(side, group):
+        at = pl.ds(pl.multiple_of((side * E + group) * span, span), span)
+        return jnp.concatenate([ys[k, at, :] for k in range(planes)], axis=1)
+
+    for d in order:
+        group = lax.rem(e + d, E)
+        y_tx[d] = summed(other, group).astype(b16)
+        yc[d] = remote(y_tx.at[d], y_rx.at[d], ys_ssem.at[d], ys_rsem.at[d], sibling)
+        yc[d].start()
+    ye = []
+    for d in order:
+        group = lax.rem(e + d, E)
+        yc[d].wait_recv()
+        both = summed(s, group) + y_rx[d].astype(f32)
+        if d:
+            z_tx[d - 1] = both.astype(b16)
+            copy = remote(z_tx.at[d - 1], z_rx.at[d - 1], ye_ssem.at[d - 1], ye_rsem.at[d - 1], e_peer(d))
+            copy.start()
+            ye.append(copy)
+        else:
+            z_all = both
+    for d in range(1, E):
+        ye[d - 1].wait_recv()
+        z_all += z_rx[d - 1].astype(f32)
+    z_sum[...] = z_all.reshape(z_sum.shape)
+    f_tx[...] = z_sum[...].astype(b16)
+    yz = [
+        remote(f_tx.at[lax.rem(r + d, R)], f_rx.at[d - 1], yz_ssem.at[d - 1], yz_rsem.at[d - 1], z_peer(d))
+        for d in range(1, R)
+    ]
+    for copy in yz:
+        copy.start()
+    sent += list(yc.values()) + ye + yz
+    pick = lax.broadcasted_iota(jnp.int32, (8, tokens), 0) + (mine * E + e) * nt
+    pick = (pick == lax.broadcasted_iota(jnp.int32, (8, tokens), 1)).astype(b16)
+    own = [
+        jnp.dot(pick, xs[c].reshape(tokens, xs.shape[3])[:, :width], preferred_element_type=f32)
+        for c in range(chunks)
+    ]
+    routed = z_sum[r]
+    for d in range(1, R):
+        yz[d - 1].wait_recv()
+        routed += f_rx[d - 1].astype(f32)
+    for c in range(chunks):
+        out_ref[:, c * width : (c + 1) * width] = (own[c][:nt] + routed[c * nt : (c + 1) * nt]).astype(b16)
+
+    for copy in sent:
+        copy.wait_send()
+    for c in range(chunks):
+        here = (r == c // S) & (s == c % S) & (e == r)
+
+        @pl.when(jnp.logical_not(here))
+        def _():
+            remote(res_tx.at[c], res_rx.at[slot], res_ssem.at[c], res_rsem.at[slot], (c // S, c % S, r)).wait_send()
+
+
+def fused(
+    dims, residual, queries, cache, blocks, lengths, value_up, out_proj, gain, router, ids, w_gate, w_up, w_down
+):
+    R, S, E = dims
+    f32, b16 = jnp.float32, jnp.bfloat16
+    drafts, heads, qk = queries.shape
+    half_heads = heads // S
+    width = out_proj.shape[1]
+    nt, model = residual.shape
+    keys_len = cache.shape[0]
+    chunks = R * S
+    lanes = -(-keys_len // 128) * 128
+    ff = w_gate.shape[1]
+    per_owner = nt * chunks
+    dma = pltpu.SemaphoreType.DMA
+    vmem, smem, hbm = (pl.BlockSpec(memory_space=m) for m in (pltpu.VMEM, pltpu.SMEM, pl.ANY))
+    scratch = [
+        pltpu.VMEM((drafts, half_heads, qk), b16),
+        pltpu.VMEM((half_heads,) + value_up.shape[1:], b16),
+        pltpu.VMEM(out_proj.shape, b16),
+        pltpu.VMEM(router.shape, b16),
+        pltpu.VMEM(w_gate.shape, b16),
+        pltpu.VMEM(w_up.shape, b16),
+        pltpu.VMEM(w_down.shape, b16),
+        pltpu.VMEM(cache.shape, b16),
+        pltpu.VMEM((2, 8, lanes), f32),
+        pltpu.VMEM((chunks, nt, width + 128), f32),
+        pltpu.VMEM((S * E, nt, width + 128), f32),
+        pltpu.VMEM((DL // 128, drafts * half_heads, 128), f32),
+        pltpu.VMEM((S, R, drafts, half_heads * DV), b16),
+        pltpu.VMEM((E, drafts, width), f32),
+        pltpu.VMEM((E, drafts, width), b16),
+        pltpu.VMEM((E - 1, drafts, width), b16),
+        pltpu.VMEM((drafts, width + 128), f32),
+        pltpu.VMEM((chunks, E, drafts, width + 128), b16),
+        pltpu.VMEM((width // 128, R * S * E * per_owner, 128), f32),
+        pltpu.VMEM((E, R * per_owner, width), b16),
+        pltpu.VMEM((E, R * per_owner, width), b16),
+        pltpu.VMEM((R, per_owner, width), f32),
+        pltpu.VMEM((E - 1, R * per_owner, width), b16),
+        pltpu.VMEM((E - 1, R * per_owner, width), b16),
+        pltpu.VMEM((R, per_owner, width), b16),
+        pltpu.VMEM((R - 1, per_owner, width), b16),
+        dma((7,)),
+        dma((2,)),
+        dma((2,)),
+        dma((chunks,)),
+        dma((S * E,)),
+        dma((R - 1,)),
+        dma((R - 1,)),
+        dma((R,)),
+        dma((R,)),
+        dma((E - 1,)),
+        dma((E - 1,)),
+        dma((R - 1,)),
+        dma((R - 1,)),
+        dma((R, E - 1)),
+        dma((R, E - 1)),
+        dma((R,)),
+        dma((R,)),
+        dma((E,)),
+        dma((E,)),
+        dma((E - 1,)),
+        dma((E - 1,)),
+        dma((R - 1,)),
+        dma((R - 1,)),
+    ]
+    return pl.pallas_call(
+        functools.partial(fused_kernel, dims),
+        out_shape=jax.ShapeDtypeStruct((nt, model), b16),
+        in_specs=[vmem, hbm, vmem, smem, smem, hbm, hbm, vmem, hbm, smem, hbm, hbm, hbm],
+        out_specs=vmem,
+        scratch_shapes=scratch,
+        compiler_params=pltpu.CompilerParams(
+            collective_id=0, has_side_effects=True, vmem_limit_bytes=56 * 1024 * 1024
+        ),
+        cost_estimate=pl.CostEstimate(
+            flops=2 * R * drafts * (out_proj.size + 3 * w_gate.size),
+            bytes_accessed=2 * (value_up.size + out_proj.size + 3 * w_gate.size),
+            transcendentals=0,
+        ),
+    )(residual, queries, cache, blocks, lengths, value_up, out_proj, gain, router, ids, w_gate, w_up, w_down)
+
+
+def per_device_fused(dims, *args):
+    (residual, queries, cache, blocks, lengths, value_up, out_proj, gain, router, ids, w_gate, w_up, w_down) = args
+    return fused(
+        dims,
+        residual,
+        queries[0],
+        cache[0],
+        blocks[0, 0],
+        lengths,
+        value_up,
+        out_proj,
+        gain[None],
+        router.T,
+        ids,
+        w_gate[0],
+        w_up[0],
+        w_down[0],
+    )
+
+
+def fits_fused(dims, shapes):
+    R, S, E = dims
+    residual, queries, cache, router = shapes[0], shapes[1], shapes[2], shapes[8]
+    drafts, heads, model = queries[1], queries[2], residual[1]
+    return (
+        S == 2
+        and R == E
+        and queries[0] == R
+        and router[1] == R
+        and drafts % 16 == 0
+        and residual[0] == R * drafts
+        and heads % (E * S * 16) == 0
+        and model % (R * S * 128) == 0
+        and (residual[0] // E) % 16 == 0
+        and (drafts // (S * E) * R * S) % 16 == 0
+        and cache[1] // S % BLOCK == 0
+    )
+
+
 def solution(mesh):
     in_specs = (
         P(("req", "seq", "exp"), None),
@@ -178,6 +672,11 @@
         P("req", ("seq", "exp"), None),
     )
     out_specs = P(("req", "seq", "exp"), None)
-    return jax.shard_map(
-        per_device, mesh=mesh, in_specs=in_specs, out_specs=out_specs, check_vma=False
-    )
+    dims = (mesh.shape["req"], mesh.shape["seq"], mesh.shape["exp"])
+
+    def layer(*args):
+        fast = fits_fused(dims, [a.shape for a in args])
+        body = functools.partial(per_device_fused, dims) if fast else per_device
+        return jax.shard_map(body, mesh=mesh, in_specs=in_specs, out_specs=out_specs, check_vma=False)(*args)
+
+    return layer

time: 119 us -> 52 us (0.44)
  Pallas kernels: 0 us -> 48.4 us
  blocking collectives: 47.1 us -> 0 us
  waiting for transfers between devices: 30.8 us -> 0 us
  matrix products: 18.1 us -> 0 us
  starting transfers between devices: 9.07 us -> 0 us
  other arithmetic: 5.23 us -> 0 us
  local copies, waits for them, and re-layouts: 6.93 us -> 2.72 us
    pallas_call x0 -> x1, Pallas kernels: none -> 48.4 us  [fused(): pl.pallas_call(functools.partial(fused_kernel, dims), out_shape=jax.Shape...]
    all_to_all x2 -> x0, waiting for transfers between devices: 30.8 us -> none  [the longest x1 23.3 us: per_device(): lax.all_to_all(expert_rows(lax.all_to_all(fanned, ('req', 'seq', 'exp'),...]
    all_to_all x1 -> x0, blocking collectives: 25.6 us -> none  [per_device(): lax.all_to_all(fanned, ('req', 'seq', 'exp'), split_axis=0, concat_axis=0...]
    all_gather x3 -> x0, blocking collectives: 21.5 us -> none  [the longest x1 17.6 us: per_device(): lax.all_gather(flat_values, 'req', axis=0, tiled=True)]
    dot_general x10 -> x0, matrix products: 18.1 us -> none  [the longest x1 5.45 us: expert_rows(): jnp.dot(activated, w_down[0], preferred_element_type=jnp.float32)]
    all_to_all x2 -> x0, starting transfers between devices: 9.07 us -> none  [the longest x1 6.01 us: per_device(): lax.all_to_all(col_terms[None].astype(jnp.bfloat16), ('req', 'seq', 'exp'...]
    reduce_sum x8 -> x0, other arithmetic: 1.94 us -> none  [the longest x1 0.79 us: per_device(): expert_out = jnp.sum(returned, 1).astype(jnp.bfloat16)]
    reshape x3 -> x0, local copies, waits for them, and re-layouts: 1.67 us -> none  [the longest x1 1.27 us: expert_rows(): return partial_value.reshape(arrived.shape)]
  transfers between devices with their start and end apart: 2 -> 0, of which waited for: 2 -> 0; matrix products, arithmetic and copies ran while one was open for 1% -> 0% of each run, Pallas kernels for 0% -> 0%
where the time goes in v1:
time: 52 us; the launch traced here: 51.8 us
  Pallas kernels  48.4 us (93%)
  local copies, waits for them, and re-layouts  2.72 us (5%)
  between operations  0.66 us (1%)
    pallas_call x1, Pallas kernels, fused(): pl.pallas_call(functools.partial(fused_kernel, dims), out_shape=jax.Shape...  48.4 us
    unnamed x1, local copies, waits for them, and re-layouts  1.38 us
    broadcast_in_dim x1, local copies, waits for them, and re-layouts, per_device_fused(): gain[None]  1.34 us

profile of v1, /device:TPU:0, one launch (start us, length us, event | category | flops | bytes accessed | tf_op | source)
XLA Modules:
  0.0 51.8 jit_solution(14814114998360436174)
XLA Ops:
  0.7 1.3 %broadcast_in_dim.3.gain_ref = bf16[1,7168]{1,0:T(2,128)(2,1)} reshape(bf16[7168]{0:T(1024)(128)(2,1)} %param.20) | data formatting | bytes 28672 | tf_op jit(solution)/shard_map/broadcast_in_dim | solution.py:630
  2.0 48.4 %shard_map.127 = bf16[2,7168]{1,0:T(2,128)(2,1)} custom-call(bf16[2,7168]{1,0:T(2,128)(2,1)} %residual_ref.1, bf16[16,32,576]{2,1,0:T(8,128)(2,1)} %bitcast.10, bf16[192,576]{1,0:T(8,128)(2,1)} %bitcast.11, s32[2]{0:T(128)} %bitcast.13, s32[1]{0:T(128)S(6)} %copy.15.lengths_ref, bf16[32,512,128]{2,1,0:T(8,128)(2,1)} %value_up_hbm.1, ...), custom_call_target="tpu_custom_call" | custom-call | flops 1174405120 | bytes 22544384 | tf_op jit(solution)/shard_map/pallas_call | solution.py:602
  50.4 1.4 %copy.16 = bf16[2,7168]{1,0:T(2,128)(2,1)} copy(bf16[2,7168]{1,0:T(2,128)(2,1)} %shard_map.127) | data formatting | bytes 57344

commit v2 on v1

--- a/solution.py
+++ b/solution.py
@@ -166,6 +166,15 @@
 
 
 MESH = pl.DeviceIdType.MESH
+
+
+def column_cuts(width):
+    return [(0, width - 256), (width - 256, width)]
+
+
+def column_groups(width):
+    cuts = column_cuts(width)
+    return [(lo, min(lo + 256, cuts[0][1])) for lo in range(0, cuts[0][1], 256)] + cuts[1:]
 
 
 def fused_kernel(
@@ -195,44 +204,39 @@
     marks,
     res_tx,
     res_rx,
+    gains,
     lat,
     hv,
     acc,
-    part_tx,
-    part_rx,
     res_sum,
+    hots,
+    ys,
+    parts_tx,
+    parts_rx,
     xs,
-    ys,
     y_tx,
     y_rx,
-    z_sum,
-    z_tx,
-    z_rx,
-    f_tx,
-    f_rx,
+    both,
+    mid_tx,
+    mid_rx,
+    mid_sum,
+    end_tx,
+    end_rx,
     load_sem,
     key_sem,
     mark_sem,
     res_ssem,
     res_rsem,
-    hz_ssem,
-    hz_rsem,
-    hs_ssem,
-    hs_rsem,
-    ps_ssem,
-    ps_rsem,
-    az_ssem,
-    az_rsem,
-    ae_ssem,
-    ae_rsem,
-    as_ssem,
-    as_rsem,
-    ys_ssem,
-    ys_rsem,
-    ye_ssem,
-    ye_rsem,
-    yz_ssem,
-    yz_rsem,
+    hz_sem,
+    hs_sem,
+    hot_sem,
+    ps_sem,
+    first_sem,
+    second_sem,
+    across_sem,
+    ys_sem,
+    mid_sem,
+    end_sem,
 ):
     R, S, E = dims
     f32, b16 = jnp.float32, jnp.bfloat16
@@ -277,6 +281,7 @@
             def _():
                 pl.semaphore_signal(barrier, inc=1, device_id=(e, ss, ee), device_id_type=MESH)
 
+    gains[...] = gain_ref[...].astype(f32).reshape(gains.shape)
     block_of = lax.broadcasted_iota(jnp.int32, marks.shape[1:], 1) // BLOCK
     hit = block_of == blocks_ref[0]
     for i in range(1, blocks_ref.shape[0]):
@@ -350,7 +355,7 @@
         hv[s, r, :, h * DV : (h + 1) * DV] = jnp.dot(one, vu_v[h], preferred_element_type=f32).astype(b16)
 
     hz = [
-        remote(hv.at[s, r], hv.at[s, r], hz_ssem.at[d - 1], hz_rsem.at[d - 1], z_peer(d)) for d in range(1, R)
+        remote(hv.at[s, r], hv.at[s, r], hz_sem.at[0, d - 1], hz_sem.at[1, d - 1], z_peer(d)) for d in range(1, R)
     ]
     for copy in hz:
         copy.start()
@@ -359,7 +364,7 @@
         if d:
             hz[d - 1].wait_recv()
         origin = lax.rem(r + R - d, R)
-        copy = remote(hv.at[s, origin], hv.at[s, origin], hs_ssem.at[d], hs_rsem.at[d], sibling)
+        copy = remote(hv.at[s, origin], hv.at[s, origin], hs_sem.at[0, d], hs_sem.at[1, d], sibling)
         copy.start()
         hs.append(copy)
     sent += hz + hs
@@ -367,60 +372,101 @@
     loads[2].wait()
     half = half_heads * DV
 
-    def out_part(side):
+    def out_part(side, lo, hi):
         head_rows = hv[side].reshape(R * drafts, half)
-        return jnp.dot(head_rows, op_v[pl.ds(pl.multiple_of(side * half, half), half), :], preferred_element_type=f32)
-
-    acc[...] = out_part(s).reshape(acc.shape)
+        depth = pl.ds(pl.multiple_of(side * half, half), half)
+        part = jnp.dot(head_rows, op_v[depth, lo:hi], preferred_element_type=f32)
+        return part.reshape(E, drafts, hi - lo)
+
+    cuts = column_cuts(width)
+    for lo, hi in cuts:
+        acc[:, :, lo:hi] = out_part(s, lo, hi)
     for j in range(S * E):
         pltpu.make_async_copy(res_rx.at[j], res_rx.at[j], res_rsem.at[j]).wait()
         res_sum[j * nt : (j + 1) * nt, :] = res_rx[j]
+    hots[e] = res_sum[:, width:].astype(b16)
+    hot_copies = [
+        remote(hots.at[e], hots.at[e], hot_sem.at[0, d - 1], hot_sem.at[1, d - 1], e_peer(d)) for d in range(1, E)
+    ]
+    for copy in hot_copies:
+        copy.start()
+    sent += hot_copies
     for copy in hs:
         copy.wait_recv()
-    acc[...] += out_part(other).reshape(acc.shape)
-    part_tx[...] = acc[...].astype(b16)
-    ps = [
-        remote(part_tx.at[lax.rem(e + d, E)], part_rx.at[d - 1], ps_ssem.at[d - 1], ps_rsem.at[d - 1], e_peer(d))
-        for d in range(1, E)
-    ]
-    for copy in ps:
-        copy.start()
-    attended = acc[e]
-    for d in range(1, E):
-        ps[d - 1].wait_recv()
-        attended += part_rx[d - 1].astype(f32)
-    sent += ps
-    hidden = res_sum[:, :width] + attended.astype(b16).astype(f32)
-    xs[mine, e, :, :width] = hidden.astype(b16)
-    xs[mine, e, :, width:] = res_sum[:, width:].astype(b16)
-
-    az = [
-        remote(xs.at[mine, e], xs.at[mine, e], az_ssem.at[d - 1], az_rsem.at[d - 1], z_peer(d)) for d in range(1, R)
-    ]
-    for copy in az:
-        copy.start()
-    ae = []
-    for dz in range(R):
-        if dz:
-            az[dz - 1].wait_recv()
-        chunk = lax.rem(r + R - dz, R) * S + s
-        row = [
-            remote(xs.at[chunk, e], xs.at[chunk, e], ae_ssem.at[dz, d - 1], ae_rsem.at[dz, d - 1], e_peer(d))
+    ps = [None, None]
+    for i in (1, 0):
+        lo, hi = cuts[i]
+        acc[:, :, lo:hi] += out_part(other, lo, hi)
+        parts_tx[i][...] = acc[:, :, lo:hi].astype(b16)
+        ps[i] = [
+            remote(
+                parts_tx[i].at[lax.rem(e + d, E)],
+                parts_rx[i].at[d - 1],
+                ps_sem.at[0, i, d - 1],
+                ps_sem.at[1, i, d - 1],
+                e_peer(d),
+            )
             for d in range(1, E)
         ]
-        for copy in row:
+        for copy in ps[i]:
             copy.start()
-        ae.append(row)
+        sent += ps[i]
+
+    def chunk_at(d):
+        return lax.rem(r + R - d, R) * S + s
+
+    def group_at(d):
+        return lax.rem(e + E - d, E)
+
+    first = [None, None]
+    for i in (1, 0):
+        lo, hi = cuts[i]
+        attended = acc[e, :, lo:hi]
+        for d in range(1, E):
+            ps[i][d - 1].wait_recv()
+            attended += parts_rx[i][d - 1].astype(f32)
+        xs[i][mine, e] = (res_sum[:, lo:hi] + attended.astype(b16).astype(f32)).astype(b16)
+        block = xs[i].at[mine, e]
+        first[i] = [
+            remote(block, block, first_sem.at[0, i, d - 1], first_sem.at[1, i, d - 1], (e_peer if i else z_peer)(d))
+            for d in range(1, E if i else R)
+        ]
+        for copy in first[i]:
+            copy.start()
+        sent += first[i]
+    second = [[], []]
+    for hop in range(max(R, E)):
+        for i in (1, 0):
+            if hop >= (E if i else R):
+                continue
+            if hop:
+                first[i][hop - 1].wait_recv()
+            block = xs[i].at[mine, group_at(hop)] if i else xs[i].at[chunk_at(hop), e]
+            row = [
+                remote(
+                    block,
+                    block,
+                    second_sem.at[0, i, hop, d - 1],
+                    second_sem.at[1, i, hop, d - 1],
+                    (z_peer if i else e_peer)(d),
+                )
+                for d in range(1, R if i else E)
+            ]
+            for copy in row:
+                copy.start()
+            second[i].append(row)
+            sent += row
     for load in loads[3:6]:
         load.wait()
 
-    tokens = E * xs.shape[2]
-
-    def expert_part(state, chunk):
+    tokens = E * drafts
+
+    def expert_part(state, chunk, i):
         squares, gate, up, logits = state
-        hid = xs[chunk].reshape(tokens, xs.shape[3])[:, :width].astype(f32)
-        cols = pl.ds(pl.multiple_of(chunk * width, width), width)
-        scaled = (hid * gain_ref[:, cols].astype(f32)).astype(b16)
+        lo, hi = cuts[i]
+        hid = xs[i][chunk].reshape(tokens, hi - lo).astype(f32)
+        cols = pl.ds(pl.multiple_of(chunk * width + lo, 128), hi - lo)
+        scaled = (hid * gains[:, cols]).astype(b16)
         return (
             squares + jnp.sum(hid * hid, -1, keepdims=True),
             gate + jnp.dot(scaled, wg_v[cols, :], preferred_element_type=f32),
@@ -435,23 +481,32 @@
         jnp.zeros((tokens, rt_v.shape[0]), f32),
     )
     across = []
-    for dz in range(R):
-        for copy in ae[dz]:
-            copy.wait_recv()
-        chunk = lax.rem(r + R - dz, R) * S + s
-        copy = remote(xs.at[chunk], xs.at[chunk], as_ssem.at[dz], as_rsem.at[dz], sibling)
-        copy.start()
-        across.append(copy)
-        state = expert_part(state, chunk)
-    for dz in range(R):
-        across[dz].wait_recv()
-        state = expert_part(state, lax.rem(r + R - dz, R) * S + other)
-    sent += az + [copy for row in ae for copy in row] + across
+    for d in range(R):
+        for i in (0, 1):
+            if i == 0:
+                waits = second[0][d]
+            elif d == 0:
+                waits = []
+            else:
+                waits = [row[d - 1] for row in second[1]]
+            for copy in waits:
+                copy.wait_recv()
+            whole = xs[i].at[chunk_at(d)]
+            copy = remote(whole, whole, across_sem.at[0, i, d], across_sem.at[1, i, d], sibling)
+            copy.start()
+            across.append(copy)
+            state = expert_part(state, chunk_at(d), i)
+    for d in range(R):
+        for i in (0, 1):
+            across[2 * d + i].wait_recv()
+            state = expert_part(state, lax.rem(r + R - d, R) * S + other, i)
+    sent += across
     squares, gate, up, logits = state
     scale = lax.rsqrt(squares / (chunks * width) + 1e-06)
     experts = rt_v.shape[0]
-    hots = xs[mine].reshape(tokens, xs.shape[3])[:, width : width + experts].astype(f32)
-    chosen = hots * jax.nn.sigmoid(logits * scale)
+    for copy in hot_copies:
+        copy.wait_recv()
+    chosen = hots[...].reshape(tokens, 128)[:, :experts].astype(f32) * jax.nn.sigmoid(logits * scale)
     this_expert = lax.broadcasted_iota(jnp.int32, (1, experts), 1) == r
     weight = jnp.sum(jnp.where(this_expert, chosen, 0.0), -1, keepdims=True)
     weight = weight / jnp.sum(chosen, -1, keepdims=True) * 2.5
@@ -464,63 +519,89 @@
     ordered = jnp.dot((wanted == from_row).astype(b16), activated, preferred_element_type=f32).astype(b16)
     loads[6].wait()
     per_owner = nt * chunks
-    planes = width // 128
-    for c in range(chunks):
-        down = jnp.dot(ordered, wd_v[:, c * width : (c + 1) * width], preferred_element_type=f32)
-        for t in range(nt):
-            part = down[t * devices : (t + 1) * devices]
-            for k in range(planes):
-                ys[k, pl.ds(c * nt + t, devices, stride=per_owner), :] = part[:, k * 128 : (k + 1) * 128]
-
-    span = R * per_owner
-    order = list(range(1, E)) + [0]
-    yc = {}
-
-    def summed(side, group):
-        at = pl.ds(pl.multiple_of((side * E + group) * span, span), span)
-        return jnp.concatenate([ys[k, at, :] for k in range(planes)], axis=1)
-
-    for d in order:
-        group = lax.rem(e + d, E)
-        y_tx[d] = summed(other, group).astype(b16)
-        yc[d] = remote(y_tx.at[d], y_rx.at[d], ys_ssem.at[d], ys_rsem.at[d], sibling)
-        yc[d].start()
-    ye = []
-    for d in order:
-        group = lax.rem(e + d, E)
-        yc[d].wait_recv()
-        both = summed(s, group) + y_rx[d].astype(f32)
-        if d:
-            z_tx[d - 1] = both.astype(b16)
-            copy = remote(z_tx.at[d - 1], z_rx.at[d - 1], ye_ssem.at[d - 1], ye_rsem.at[d - 1], e_peer(d))
+    groups = column_groups(width)
+    order = [len(groups) - 1] + list(range(len(groups) - 1))
+    half_rows = R * E * per_owner
+
+    def summed(side, lo, hi):
+        at = pl.ds(pl.multiple_of(side * half_rows, half_rows), half_rows)
+        part = jnp.concatenate([ys[k, at, :] for k in range(lo // 128, hi // 128)], axis=1)
+        return part.reshape(E, R, per_owner, hi - lo)
+
+    with_core, mid, end = {}, {}, {}
+
+    def peers_of(g):
+        return (z_peer, r, R, e_peer, e, E) if g == len(groups) - 1 else (e_peer, e, E, z_peer, r, R)
+
+    def begin(g):
+        lo, hi = groups[g]
+        for c in range(chunks):
+            down = jnp.dot(ordered, wd_v[:, c * width + lo : c * width + hi], preferred_element_type=f32)
+            for t in range(nt):
+                part = down[t * devices : (t + 1) * devices]
+                for k in range(lo // 128, hi // 128):
+                    column = part[:, k * 128 - lo : (k + 1) * 128 - lo]
+                    ys[k, pl.ds(c * nt + t, devices, stride=per_owner), :] = column
+        y_tx[g][...] = summed(other, lo, hi).astype(b16)
+        with_core[g] = remote(y_tx[g], y_rx[g], ys_sem.at[0, g], ys_sem.at[1, g], sibling)
+        with_core[g].start()
+
+    def middle(g):
+        lo, hi = groups[g]
+        peer, me, count = peers_of(g)[:3]
+        with_core[g].wait_recv()
+        both[g][...] = summed(s, lo, hi) + y_rx[g][...].astype(f32)
+        mid[g] = []
+        for d in range(1, count):
+            to = lax.rem(me + d, count)
+            block = both[g][:, to] if g == len(groups) - 1 else both[g][to]
+            mid_tx[g][d - 1] = block.astype(b16)
+            copy = remote(
+                mid_tx[g].at[d - 1], mid_rx[g].at[d - 1], mid_sem.at[0, g, d - 1], mid_sem.at[1, g, d - 1], peer(d)
+            )
             copy.start()
-            ye.append(copy)
-        else:
-            z_all = both
-    for d in range(1, E):
-        ye[d - 1].wait_recv()
-        z_all += z_rx[d - 1].astype(f32)
-    z_sum[...] = z_all.reshape(z_sum.shape)
-    f_tx[...] = z_sum[...].astype(b16)
-    yz = [
-        remote(f_tx.at[lax.rem(r + d, R)], f_rx.at[d - 1], yz_ssem.at[d - 1], yz_rsem.at[d - 1], z_peer(d))
-        for d in range(1, R)
-    ]
-    for copy in yz:
-        copy.start()
-    sent += list(yc.values()) + ye + yz
+            mid[g].append(copy)
+
+    for n, g in enumerate(order):
+        begin(g)
+        if n:
+            middle(order[n - 1])
+    middle(order[-1])
+    for g in order:
+        peer, me, count = peers_of(g)[3:]
+        total_g = both[g][:, r] if g == len(groups) - 1 else both[g][e]
+        for d, copy in enumerate(mid[g]):
+            copy.wait_recv()
+            total_g += mid_rx[g][d].astype(f32)
+        mid_sum[g][...] = total_g
+        end_tx[g][...] = total_g.astype(b16)
+        end[g] = []
+        for d in range(1, count):
+            to = lax.rem(me + d, count)
+            copy = remote(
+                end_tx[g].at[to], end_rx[g].at[d - 1], end_sem.at[0, g, d - 1], end_sem.at[1, g, d - 1], peer(d)
+            )
+            copy.start()
+            end[g].append(copy)
+        sent += [with_core[g]] + mid[g] + end[g]
     pick = lax.broadcasted_iota(jnp.int32, (8, tokens), 0) + (mine * E + e) * nt
     pick = (pick == lax.broadcasted_iota(jnp.int32, (8, tokens), 1)).astype(b16)
-    own = [
-        jnp.dot(pick, xs[c].reshape(tokens, xs.shape[3])[:, :width], preferred_element_type=f32)
-        for c in range(chunks)
-    ]
-    routed = z_sum[r]
-    for d in range(1, R):
-        yz[d - 1].wait_recv()
-        routed += f_rx[d - 1].astype(f32)
+    own = []
     for c in range(chunks):
-        out_ref[:, c * width : (c + 1) * width] = (own[c][:nt] + routed[c * nt : (c + 1) * nt]).astype(b16)
+        sides = [
+            jnp.dot(pick, xs[i][c].reshape(tokens, hi - lo), preferred_element_type=f32)
+            for i, (lo, hi) in enumerate(cuts)
+        ]
+        own.append(jnp.concatenate(sides, axis=1))
+    for g in order:
+        lo, hi = groups[g]
+        routed = mid_sum[g][peers_of(g)[4]]
+        for d, copy in enumerate(end[g]):
+            copy.wait_recv()
+            routed += end_rx[g][d].astype(f32)
+        for c in range(chunks):
+            value = own[c][:nt, lo:hi] + routed[c * nt : (c + 1) * nt]
+            out_ref[:, c * width + lo : c * width + hi] = value.astype(b16)
 
     for copy in sent:
         copy.wait_send()
@@ -546,6 +627,7 @@
     lanes = -(-keys_len // 128) * 128
     ff = w_gate.shape[1]
     per_owner = nt * chunks
+    cuts, groups = column_cuts(width), column_groups(width)
     dma = pltpu.SemaphoreType.DMA
     vmem, smem, hbm = (pl.BlockSpec(memory_space=m) for m in (pltpu.VMEM, pltpu.SMEM, pl.ANY))
     scratch = [
@@ -560,44 +642,39 @@
         pltpu.VMEM((2, 8, lanes), f32),
         pltpu.VMEM((chunks, nt, width + 128), f32),
         pltpu.VMEM((S * E, nt, width + 128), f32),
+        pltpu.VMEM((1, model), f32),
         pltpu.VMEM((DL // 128, drafts * half_heads, 128), f32),
         pltpu.VMEM((S, R, drafts, half_heads * DV), b16),
         pltpu.VMEM((E, drafts, width), f32),
-        pltpu.VMEM((E, drafts, width), b16),
-        pltpu.VMEM((E - 1, drafts, width), b16),
         pltpu.VMEM((drafts, width + 128), f32),
-        pltpu.VMEM((chunks, E, drafts, width + 128), b16),
+        pltpu.VMEM((E, drafts, 128), b16),
         pltpu.VMEM((width // 128, R * S * E * per_owner, 128), f32),
-        pltpu.VMEM((E, R * per_owner, width), b16),
-        pltpu.VMEM((E, R * per_owner, width), b16),
-        pltpu.VMEM((R, per_owner, width), f32),
-        pltpu.VMEM((E - 1, R * per_owner, width), b16),
-        pltpu.VMEM((E - 1, R * per_owner, width), b16),
-        pltpu.VMEM((R, per_owner, width), b16),
-        pltpu.VMEM((R - 1, per_owner, width), b16),
+        [pltpu.VMEM((E, drafts, hi - lo), b16) for lo, hi in cuts],
+        [pltpu.VMEM((E - 1, drafts, hi - lo), b16) for lo, hi in cuts],
+        [pltpu.VMEM((chunks, E, drafts, hi - lo), b16) for lo, hi in cuts],
+        [pltpu.VMEM((E, R, per_owner, hi - lo), b16) for lo, hi in groups],
+        [pltpu.VMEM((E, R, per_owner, hi - lo), b16) for lo, hi in groups],
+        [pltpu.VMEM((E, R, per_owner, hi - lo), f32) for lo, hi in groups],
+        [pltpu.VMEM((E - 1, R, per_owner, hi - lo), b16) for lo, hi in groups],
+        [pltpu.VMEM((E - 1, R, per_owner, hi - lo), b16) for lo, hi in groups],
+        [pltpu.VMEM((R, per_owner, hi - lo), f32) for lo, hi in groups],
+        [pltpu.VMEM((R, per_owner, hi - lo), b16) for lo, hi in groups],
+        [pltpu.VMEM((R - 1, per_owner, hi - lo), b16) for lo, hi in groups],
         dma((7,)),
         dma((2,)),
         dma((2,)),
         dma((chunks,)),
         dma((S * E,)),
-        dma((R - 1,)),
-        dma((R - 1,)),
-        dma((R,)),
-        dma((R,)),
-        dma((E - 1,)),
-        dma((E - 1,)),
-        dma((R - 1,)),
-        dma((R - 1,)),
-        dma((R, E - 1)),
-        dma((R, E - 1)),
-        dma((R,)),
-        dma((R,)),
-        dma((E,)),
-        dma((E,)),
-        dma((E - 1,)),
-        dma((E - 1,)),
-        dma((R - 1,)),
-        dma((R - 1,)),
+        dma((2, R - 1)),
+        dma((2, R)),
+        dma((2, E - 1)),
+        dma((2, 2, E - 1)),
+        dma((2, 2, R - 1)),
+        dma((2, 2, R, E - 1)),
+        dma((2, 2, R)),
+        dma((2, len(groups))),
+        dma((2, len(groups), E - 1)),
+        dma((2, len(groups), E - 1)),
     ]
     return pl.pallas_call(
         functools.partial(fused_kernel, dims),
@@ -627,7 +704,7 @@
         lengths,
         value_up,
         out_proj,
-        gain[None],
+        gain,
         router.T,
         ids,
         w_gate[0],
@@ -649,6 +726,7 @@
         and residual[0] == R * drafts
         and heads % (E * S * 16) == 0
         and model % (R * S * 128) == 0
+        and model // (R * S) >= 384
         and (residual[0] // E) % 16 == 0
         and (drafts // (S * E) * R * S) % 16 == 0
         and cache[1] // S % BLOCK == 0

time: 52 us -> 48.9 us (0.940)
  Pallas kernels: 48.4 us -> 46.7 us
  local copies, waits for them, and re-layouts: 2.72 us -> 1.38 us
    pallas_call x1, Pallas kernels: 48.4 us -> 46.7 us  [fused(): pl.pallas_call(functools.partial(fused_kernel, dims), out_shape=jax.Shape...]
    broadcast_in_dim x1 -> x0, local copies, waits for them, and re-layouts: 1.34 us -> none  [per_device_fused(): gain[None]]
where the time goes in v2:
time: 48.9 us; the launch traced here: 48.7 us
  Pallas kernels  46.7 us (96%)
  local copies, waits for them, and re-layouts  1.38 us (3%)
  between operations  0.66 us (1%)
    pallas_call x1, Pallas kernels, fused(): pl.pallas_call(functools.partial(fused_kernel, dims), out_shape=jax.Shape...  46.7 us
    unnamed x1, local copies, waits for them, and re-layouts  1.38 us

profile of v2, /device:TPU:0, one launch (start us, length us, event | category | flops | bytes accessed | tf_op | source)
XLA Modules:
  0.0 48.7 jit_solution(12505601175538282893)
XLA Ops:
  0.7 46.7 %shard_map.127 = bf16[2,7168]{1,0:T(2,128)(2,1)} custom-call(bf16[2,7168]{1,0:T(2,128)(2,1)} %residual_ref.1, bf16[16,32,576]{2,1,0:T(8,128)(2,1)} %bitcast.10, bf16[192,576]{1,0:T(8,128)(2,1)} %bitcast.11, s32[2]{0:T(128)} %bitcast.13, s32[1]{0:T(128)S(6)} %copy.15.lengths_ref, bf16[32,512,128]{2,1,0:T(8,128)(2,1)} %value_up_hbm.1, ...), custom_call_target="tpu_custom_call" | custom-call | flops 1174405120 | bytes 22544384 | tf_op jit(solution)/shard_map/pallas_call | solution.py:679
  47.3 1.4 %copy.16 = bf16[2,7168]{1,0:T(2,128)(2,1)} copy(bf16[2,7168]{1,0:T(2,128)(2,1)} %shard_map.127) | data formatting | bytes 57344

commit v3 on v2

--- a/solution.py
+++ b/solution.py
@@ -348,39 +348,50 @@
     for k in range(lat.shape[0]):
         lat[k] = latent[:, k * 128 : (k + 1) * 128]
 
+    pieces = hv.shape[1]
+    piece_heads = half_heads // pieces
+    depth = piece_heads * DV
     loads[1].wait()
-    for h in range(half_heads):
-        one = [lat[k, pl.ds(h, drafts, stride=half_heads), :] for k in range(lat.shape[0])]
-        one = jnp.concatenate(one, axis=1).astype(b16)
-        hv[s, r, :, h * DV : (h + 1) * DV] = jnp.dot(one, vu_v[h], preferred_element_type=f32).astype(b16)
-
-    hz = [
-        remote(hv.at[s, r], hv.at[s, r], hz_sem.at[0, d - 1], hz_sem.at[1, d - 1], z_peer(d)) for d in range(1, R)
-    ]
-    for copy in hz:
-        copy.start()
+    hz = []
+    for p in range(pieces):
+        for n in range(piece_heads):
+            h = p * piece_heads + n
+            one = [lat[k, pl.ds(h, drafts, stride=half_heads), :] for k in range(lat.shape[0])]
+            one = jnp.concatenate(one, axis=1).astype(b16)
+            value = jnp.dot(one, vu_v[h], preferred_element_type=f32)
+            hv[s, p, r, :, n * DV : (n + 1) * DV] = value.astype(b16)
+        block = hv.at[s, p, r]
+        hz.append(
+            [remote(block, block, hz_sem.at[0, p, d - 1], hz_sem.at[1, p, d - 1], z_peer(d)) for d in range(1, R)]
+        )
+        for copy in hz[p]:
+            copy.start()
+        sent += hz[p]
+
+    cuts = column_cuts(width)
+    loads[2].wait()
+
+    def out_part(side, p, lo, hi):
+        head_rows = hv[side, p].reshape(R * drafts, depth)
+        at = pl.ds(pl.multiple_of((side * pieces + p) * depth, depth), depth)
+        part = jnp.dot(head_rows, op_v[at, lo:hi], preferred_element_type=f32)
+        return part.reshape(E, drafts, hi - lo)
+
     hs = []
-    for d in range(R):
-        if d:
-            hz[d - 1].wait_recv()
-        origin = lax.rem(r + R - d, R)
-        copy = remote(hv.at[s, origin], hv.at[s, origin], hs_sem.at[0, d], hs_sem.at[1, d], sibling)
-        copy.start()
-        hs.append(copy)
-    sent += hz + hs
-
-    loads[2].wait()
-    half = half_heads * DV
-
-    def out_part(side, lo, hi):
-        head_rows = hv[side].reshape(R * drafts, half)
-        depth = pl.ds(pl.multiple_of(side * half, half), half)
-        part = jnp.dot(head_rows, op_v[depth, lo:hi], preferred_element_type=f32)
-        return part.reshape(E, drafts, hi - lo)
-
-    cuts = column_cuts(width)
-    for lo, hi in cuts:
-        acc[:, :, lo:hi] = out_part(s, lo, hi)
+    for p in range(pieces):
+        for copy in hz[p]:
+            copy.wait_recv()
+        whole = hv.at[s, p]
+        hs.append(remote(whole, whole, hs_sem.at[0, p], hs_sem.at[1, p], sibling))
+        hs[p].start()
+        part = out_part(s, p, 0, width)
+        if p:
+            hs[p - 1].wait_recv()
+            part += out_part(other, p - 1, 0, width)
+            acc[...] += part
+        else:
+            acc[...] = part
+    sent += hs
     for j in range(S * E):
         pltpu.make_async_copy(res_rx.at[j], res_rx.at[j], res_rsem.at[j]).wait()
         res_sum[j * nt : (j + 1) * nt, :] = res_rx[j]
@@ -391,12 +402,11 @@
     for copy in hot_copies:
         copy.start()
     sent += hot_copies
-    for copy in hs:
-        copy.wait_recv()
+    hs[-1].wait_recv()
     ps = [None, None]
     for i in (1, 0):
         lo, hi = cuts[i]
-        acc[:, :, lo:hi] += out_part(other, lo, hi)
+        acc[:, :, lo:hi] += out_part(other, pieces - 1, lo, hi)
         parts_tx[i][...] = acc[:, :, lo:hi].astype(b16)
         ps[i] = [
             remote(
@@ -481,6 +491,13 @@
         jnp.zeros((tokens, rt_v.shape[0]), f32),
     )
     across = []
+
+    def arrived(state, d):
+        for i in (0, 1):
+            across[2 * d + i].wait_recv()
+            state = expert_part(state, lax.rem(r + R - d, R) * S + other, i)
+        return state
+
     for d in range(R):
         for i in (0, 1):
             if i == 0:
@@ -496,10 +513,9 @@
             copy.start()
             across.append(copy)
             state = expert_part(state, chunk_at(d), i)
-    for d in range(R):
-        for i in (0, 1):
-            across[2 * d + i].wait_recv()
-            state = expert_part(state, lax.rem(r + R - d, R) * S + other, i)
+        if d:
+            state = arrived(state, d - 1)
+    state = arrived(state, R - 1)
     sent += across
     squares, gate, up, logits = state
     scale = lax.rsqrt(squares / (chunks * width) + 1e-06)
@@ -628,6 +644,7 @@
     ff = w_gate.shape[1]
     per_owner = nt * chunks
     cuts, groups = column_cuts(width), column_groups(width)
+    pieces = 4
     dma = pltpu.SemaphoreType.DMA
     vmem, smem, hbm = (pl.BlockSpec(memory_space=m) for m in (pltpu.VMEM, pltpu.SMEM, pl.ANY))
     scratch = [
@@ -644,7 +661,7 @@
         pltpu.VMEM((S * E, nt, width + 128), f32),
         pltpu.VMEM((1, model), f32),
         pltpu.VMEM((DL // 128, drafts * half_heads, 128), f32),
-        pltpu.VMEM((S, R, drafts, half_heads * DV), b16),
+        pltpu.VMEM((S, pieces, R, drafts, half_heads // pieces * DV), b16),
         pltpu.VMEM((E, drafts, width), f32),
         pltpu.VMEM((drafts, width + 128), f32),
         pltpu.VMEM((E, drafts, 128), b16),
@@ -665,8 +682,8 @@
         dma((2,)),
         dma((chunks,)),
         dma((S * E,)),
-        dma((2, R - 1)),
-        dma((2, R)),
+        dma((2, pieces, R - 1)),
+        dma((2, pieces)),
         dma((2, E - 1)),
         dma((2, 2, E - 1)),
         dma((2, 2, R - 1)),

time: 48.9 us -> 48.3 us (0.988)
  Pallas kernels: 46.7 us -> 46 us
    pallas_call x1, Pallas kernels: 46.7 us -> 46 us  [fused(): pl.pallas_call(functools.partial(fused_kernel, dims), out_shape=jax.Shape...]
where the time goes in v3:
time: 48.3 us; the launch traced here: 48.1 us
  Pallas kernels  46 us (95%)
  local copies, waits for them, and re-layouts  1.38 us (3%)
  between operations  0.66 us (1%)
    pallas_call x1, Pallas kernels, fused(): pl.pallas_call(functools.partial(fused_kernel, dims), out_shape=jax.Shape...  46 us
    unnamed x1, local copies, waits for them, and re-layouts  1.38 us

profile of v3, /device:TPU:0, one launch (start us, length us, event | category | flops | bytes accessed | tf_op | source)
XLA Modules:
  0.0 48.1 jit_solution(2237950899092443346)
XLA Ops:
  0.7 46.0 %shard_map.127 = bf16[2,7168]{1,0:T(2,128)(2,1)} custom-call(bf16[2,7168]{1,0:T(2,128)(2,1)} %residual_ref.1, bf16[16,32,576]{2,1,0:T(8,128)(2,1)} %bitcast.10, bf16[192,576]{1,0:T(8,128)(2,1)} %bitcast.11, s32[2]{0:T(128)} %bitcast.13, s32[1]{0:T(128)S(6)} %copy.15.lengths_ref, bf16[32,512,128]{2,1,0:T(8,128)(2,1)} %value_up_hbm.1, ...), custom_call_target="tpu_custom_call" | custom-call | flops 1174405120 | bytes 22544384 | tf_op jit(solution)/shard_map/pallas_call | solution.py:696
  46.7 1.4 %copy.16 = bf16[2,7168]{1,0:T(2,128)(2,1)} copy(bf16[2,7168]{1,0:T(2,128)(2,1)} %shard_map.127) | data formatting | bytes 57344

commit v4 on v3

--- a/solution.py
+++ b/solution.py
@@ -177,11 +177,20 @@
     return [(lo, min(lo + 256, cuts[0][1])) for lo in range(0, cuts[0][1], 256)] + cuts[1:]
 
 
+def flipped(index, mask):
+    bit = 1
+    while bit <= mask:
+        if mask & bit:
+            index = index + bit - 2 * bit * lax.rem(lax.div(index, bit), 2)
+        bit *= 2
+    return index
+
+
 def fused_kernel(
     dims,
     residual_ref,
     queries_hbm,
-    cache_ref,
+    cache_hbm,
     blocks_ref,
     lengths_ref,
     value_up_hbm,
@@ -200,6 +209,7 @@
     wg_v,
     wu_v,
     wd_v,
+    keys_own,
     keys_rx,
     marks,
     res_tx,
@@ -244,7 +254,7 @@
     other = 1 - s
     sibling = (r, other, e)
     drafts, half_heads, _ = q_v.shape
-    keys_len = cache_ref.shape[0]
+    keys_len = cache_hbm.shape[0]
     width = op_v.shape[1]
     chunks = R * S
     nt = residual_ref.shape[0]
@@ -262,14 +272,16 @@
         pltpu.make_async_copy(w_up_hbm, wu_v, load_sem.at[5]),
         pltpu.make_async_copy(w_down_hbm, wd_v, load_sem.at[6]),
     ]
-    for load in loads:
+    keys_copy = pltpu.make_async_copy(cache_hbm, keys_own, load_sem.at[7])
+    keys_copy.start()
+    for load in loads[:2]:
         load.start()
 
     def z_peer(d):
-        return (lax.rem(r + d, R), s, e)
+        return (flipped(r, d), s, e)
 
     def e_peer(d):
-        return (r, s, lax.rem(e + d, E))
+        return (r, s, flipped(e, d))
 
     barrier = pltpu.get_barrier_semaphore()
     for peer in [sibling] + [z_peer(d) for d in range(1, R)] + [e_peer(d) for d in range(1, E)]:
@@ -281,22 +293,11 @@
             def _():
                 pl.semaphore_signal(barrier, inc=1, device_id=(e, ss, ee), device_id_type=MESH)
 
-    gains[...] = gain_ref[...].astype(f32).reshape(gains.shape)
     block_of = lax.broadcasted_iota(jnp.int32, marks.shape[1:], 1) // BLOCK
     hit = block_of == blocks_ref[0]
     for i in range(1, blocks_ref.shape[0]):
         hit = hit | (block_of == blocks_ref[i])
     marks[0] = hit.astype(f32)
-    lane = lax.broadcasted_iota(jnp.int32, (1, 128), 1)
-    for t in range(nt):
-        hot = lane == ids_ref[t, 0]
-        for k in range(1, ids_ref.shape[1]):
-            hot = hot | (lane == ids_ref[t, k])
-        for c in range(chunks):
-            res_tx[c, t : t + 1, width:] = hot.astype(f32)
-    for c in range(chunks):
-        res_tx[c, :, :width] = residual_ref[:, c * width : (c + 1) * width].astype(f32)
-
     pl.semaphore_wait(barrier, 1 + (R - 1) + (E - 1) + S * E - at_home)
 
     def remote(src, dst, ssem, rsem, peer):
@@ -305,25 +306,13 @@
         )
 
     sent = []
-    key_copy = remote(cache_ref, keys_rx, key_sem.at[0], key_sem.at[1], sibling)
+    key_copy = remote(cache_hbm, keys_rx, key_sem.at[0], key_sem.at[1], sibling)
     mark_copy = remote(marks.at[0], marks.at[1], mark_sem.at[0], mark_sem.at[1], sibling)
     key_copy.start()
     mark_copy.start()
     sent += [key_copy, mark_copy]
-    slot = s * E + e
-    for c in range(chunks):
-        to = (c // S, c % S, r)
-        here = (r == c // S) & (s == c % S) & (e == r)
-
-        @pl.when(jnp.logical_not(here))
-        def _():
-            remote(res_tx.at[c], res_rx.at[slot], res_ssem.at[c], res_rsem.at[slot], to).start()
-
-        @pl.when(here)
-        def _():
-            pltpu.make_async_copy(res_tx.at[c], res_rx.at[slot], res_rsem.at[slot]).start()
-
     loads[0].wait()
+    keys_copy.wait()
     q2 = q_v[...].reshape(drafts * half_heads, q_v.shape[2])
     rows = drafts * half_heads
     limit = lengths_ref[0] - (drafts - 1) + lax.broadcasted_iota(jnp.int32, (rows, 1), 0) // half_heads
@@ -334,7 +323,9 @@
         usable = (pos < limit) & (mark > 0)
         return jnp.where(usable, sc * (DV + DR) ** (-0.5), -1e30), usable
 
-    near, near_ok = scores_of(cache_ref[...], marks[0, :1, :keys_len], s)
+    near, near_ok = scores_of(keys_own[...], marks[0, :1, :keys_len], s)
+    for load in loads[2:]:
+        load.start()
     key_copy.wait_recv()
     mark_copy.wait_recv()
     far, far_ok = scores_of(keys_rx[...], marks[1, :1, :keys_len], other)
@@ -342,7 +333,7 @@
     near_p = jnp.where(near_ok, jnp.exp(near - top), 0.0).astype(b16)
     far_p = jnp.where(far_ok, jnp.exp(far - top), 0.0).astype(b16)
     total = jnp.sum(near_p.astype(f32), -1, keepdims=True) + jnp.sum(far_p.astype(f32), -1, keepdims=True)
-    weighted = jnp.dot(near_p, cache_ref[:, :DL], preferred_element_type=f32)
+    weighted = jnp.dot(near_p, keys_own[:, :DL], preferred_element_type=f32)
     weighted += jnp.dot(far_p, keys_rx[:, :DL], preferred_element_type=f32)
     latent = weighted / total
     for k in range(lat.shape[0]):
@@ -367,6 +358,29 @@
         for copy in hz[p]:
             copy.start()
         sent += hz[p]
+
+    gains[...] = gain_ref[...].astype(f32).reshape(gains.shape)
+    lane = lax.broadcasted_iota(jnp.int32, (1, 128), 1)
+    for t in range(nt):
+        hot = lane == ids_ref[t, 0]
+        for k in range(1, ids_ref.shape[1]):
+            hot = hot | (lane == ids_ref[t, k])
+        for c in range(chunks):
+            res_tx[c, t : t + 1, width:] = hot.astype(f32)
+    for c in range(chunks):
+        res_tx[c, :, :width] = residual_ref[:, c * width : (c + 1) * width].astype(f32)
+    slot = s * E + e
+    for c in range(chunks):
+        to = (c // S, c % S, r)
+        here = (r == c // S) & (s == c % S) & (e == r)
+
+        @pl.when(jnp.logical_not(here))
+        def _():
+            remote(res_tx.at[c], res_rx.at[slot], res_ssem.at[c], res_rsem.at[slot], to).start()
+
+        @pl.when(here)
+        def _():
+            pltpu.make_async_copy(res_tx.at[c], res_rx.at[slot], res_rsem.at[slot]).start()
 
     cuts = column_cuts(width)
     loads[2].wait()
@@ -410,7 +424,7 @@
         parts_tx[i][...] = acc[:, :, lo:hi].astype(b16)
         ps[i] = [
             remote(
-                parts_tx[i].at[lax.rem(e + d, E)],
+                parts_tx[i].at[flipped(e, d)],
                 parts_rx[i].at[d - 1],
                 ps_sem.at[0, i, d - 1],
                 ps_sem.at[1, i, d - 1],
@@ -423,10 +437,10 @@
         sent += ps[i]
 
     def chunk_at(d):
-        return lax.rem(r + R - d, R) * S + s
+        return flipped(r, d) * S + s
 
     def group_at(d):
-        return lax.rem(e + E - d, E)
+        return flipped(e, d)
 
     first = [None, None]
     for i in (1, 0):
@@ -495,7 +509,7 @@
     def arrived(state, d):
         for i in (0, 1):
             across[2 * d + i].wait_recv()
-            state = expert_part(state, lax.rem(r + R - d, R) * S + other, i)
+            state = expert_part(state, flipped(r, d) * S + other, i)
         return state
 
     for d in range(R):
@@ -569,7 +583,7 @@
         both[g][...] = summed(s, lo, hi) + y_rx[g][...].astype(f32)
         mid[g] = []
         for d in range(1, count):
-            to = lax.rem(me + d, count)
+            to = flipped(me, d)
             block = both[g][:, to] if g == len(groups) - 1 else both[g][to]
             mid_tx[g][d - 1] = block.astype(b16)
             copy = remote(
@@ -593,7 +607,7 @@
         end_tx[g][...] = total_g.astype(b16)
         end[g] = []
         for d in range(1, count):
-            to = lax.rem(me + d, count)
+            to = flipped(me, d)
             copy = remote(
                 end_tx[g].at[to], end_rx[g].at[d - 1], end_sem.at[0, g, d - 1], end_sem.at[1, g, d - 1], peer(d)
             )
@@ -656,6 +670,7 @@
         pltpu.VMEM(w_up.shape, b16),
         pltpu.VMEM(w_down.shape, b16),
         pltpu.VMEM(cache.shape, b16),
+        pltpu.VMEM(cache.shape, b16),
         pltpu.VMEM((2, 8, lanes), f32),
         pltpu.VMEM((chunks, nt, width + 128), f32),
         pltpu.VMEM((S * E, nt, width + 128), f32),
@@ -677,7 +692,7 @@
         [pltpu.VMEM((R, per_owner, hi - lo), f32) for lo, hi in groups],
         [pltpu.VMEM((R, per_owner, hi - lo), b16) for lo, hi in groups],
         [pltpu.VMEM((R - 1, per_owner, hi - lo), b16) for lo, hi in groups],
-        dma((7,)),
+        dma((8,)),
         dma((2,)),
         dma((2,)),
         dma((chunks,)),
@@ -696,7 +711,7 @@
     return pl.pallas_call(
         functools.partial(fused_kernel, dims),
         out_shape=jax.ShapeDtypeStruct((nt, model), b16),
-        in_specs=[vmem, hbm, vmem, smem, smem, hbm, hbm, vmem, hbm, smem, hbm, hbm, hbm],
+        in_specs=[vmem, hbm, hbm, smem, smem, hbm, hbm, vmem, hbm, smem, hbm, hbm, hbm],
         out_specs=vmem,
         scratch_shapes=scratch,
         compiler_params=pltpu.CompilerParams(
@@ -737,6 +752,7 @@
     return (
         S == 2
         and R == E
+        and R & (R - 1) == 0
         and queries[0] == R
         and router[1] == R
         and drafts % 16 == 0

time: 48.3 us -> 49 us (1.014)
  Pallas kernels: 46 us -> 46.7 us
    pallas_call x1, Pallas kernels: 46 us -> 46.7 us  [fused(): pl.pallas_call(functools.partial(fused_kernel, dims), out_shape=jax.Shape...]
where the time goes in v4:
time: 49 us; the launch traced here: 48.8 us
  Pallas kernels  46.7 us (95%)
  local copies, waits for them, and re-layouts  1.38 us (3%)
  between operations  0.66 us (1%)
    pallas_call x1, Pallas kernels, fused(): pl.pallas_call(functools.partial(fused_kernel, dims), out_shape=jax.Shape...  46.7 us
    unnamed x1, local copies, waits for them, and re-layouts  1.38 us

profile of v4, /device:TPU:0, one launch (start us, length us, event | category | flops | bytes accessed | tf_op | source)
XLA Modules:
  0.0 48.8 jit_solution(18298464507367422547)
XLA Ops:
  0.7 46.7 %shard_map.127 = bf16[2,7168]{1,0:T(2,128)(2,1)} custom-call(bf16[2,7168]{1,0:T(2,128)(2,1)} %residual_ref.1, bf16[16,32,576]{2,1,0:T(8,128)(2,1)} %bitcast.10, bf16[192,576]{1,0:T(8,128)(2,1)} %bitcast.11, s32[2]{0:T(128)} %bitcast.13, s32[1]{0:T(128)S(6)} %copy.15.lengths_ref, bf16[32,512,128]{2,1,0:T(8,128)(2,1)} %value_up_hbm.1, ...), custom_call_target="tpu_custom_call" | custom-call | flops 1174405120 | bytes 22544384 | tf_op jit(solution)/shard_map/pallas_call | solution.py:711
  47.4 1.4 %copy.16 = bf16[2,7168]{1,0:T(2,128)(2,1)} copy(bf16[2,7168]{1,0:T(2,128)(2,1)} %shard_map.127) | data formatting | bytes 57344

commit v5 on v3

--- a/solution.py
+++ b/solution.py
@@ -205,6 +205,9 @@
     res_tx,
     res_rx,
     gains,
+    squares,
+    gate_up,
+    logits,
     lat,
     hv,
     acc,
@@ -352,46 +355,53 @@
     piece_heads = half_heads // pieces
     depth = piece_heads * DV
     loads[1].wait()
-    hz = []
-    for p in range(pieces):
+
+    def hz_copy(p, d):
+        block = hv.at[s, p, r]
+        return remote(block, block, hz_sem.at[0, p, d - 1], hz_sem.at[1, p, d - 1], z_peer(d))
+
+    def hs_copy(p):
+        whole = hv.at[s, p]
+        return remote(whole, whole, hs_sem.at[0, p], hs_sem.at[1, p], sibling)
+
+    @pl.loop(0, pieces)
+    def _(p):
         for n in range(piece_heads):
             h = p * piece_heads + n
             one = [lat[k, pl.ds(h, drafts, stride=half_heads), :] for k in range(lat.shape[0])]
             one = jnp.concatenate(one, axis=1).astype(b16)
             value = jnp.dot(one, vu_v[h], preferred_element_type=f32)
             hv[s, p, r, :, n * DV : (n + 1) * DV] = value.astype(b16)
-        block = hv.at[s, p, r]
-        hz.append(
-            [remote(block, block, hz_sem.at[0, p, d - 1], hz_sem.at[1, p, d - 1], z_peer(d)) for d in range(1, R)]
-        )
-        for copy in hz[p]:
-            copy.start()
-        sent += hz[p]
+        for d in range(1, R):
+            hz_copy(p, d).start()
+
+    sent += [hz_copy(p, d) for p in range(pieces) for d in range(1, R)] + [hs_copy(p) for p in range(pieces)]
 
     cuts = column_cuts(width)
     loads[2].wait()
-
-    def out_part(side, p, lo, hi):
+    acc[...] = jnp.zeros_like(acc)
+
+    @pl.loop(0, 2 * pieces)
+    def _(step):
+        p = step // 2
+        near_turn = step % 2 == 0
+
+        @pl.when(near_turn)
+        def _():
+            for d in range(1, R):
+                hz_copy(p, d).wait_recv()
+            hs_copy(p).start()
+
+        @pl.when(jnp.logical_not(near_turn))
+        def _():
+            hs_copy(p).wait_recv()
+
+        side = lax.rem(s + step, 2)
         head_rows = hv[side, p].reshape(R * drafts, depth)
         at = pl.ds(pl.multiple_of((side * pieces + p) * depth, depth), depth)
-        part = jnp.dot(head_rows, op_v[at, lo:hi], preferred_element_type=f32)
-        return part.reshape(E, drafts, hi - lo)
-
-    hs = []
-    for p in range(pieces):
-        for copy in hz[p]:
-            copy.wait_recv()
-        whole = hv.at[s, p]
-        hs.append(remote(whole, whole, hs_sem.at[0, p], hs_sem.at[1, p], sibling))
-        hs[p].start()
-        part = out_part(s, p, 0, width)
-        if p:
-            hs[p - 1].wait_recv()
-            part += out_part(other, p - 1, 0, width)
-            acc[...] += part
-        else:
-            acc[...] = part
-    sent += hs
+        part = jnp.dot(head_rows, op_v[at, :], preferred_element_type=f32)
+        acc[...] += part.reshape(E, drafts, width)
+
     for j in range(S * E):
         pltpu.make_async_copy(res_rx.at[j], res_rx.at[j], res_rsem.at[j]).wait()
         res_sum[j * nt : (j + 1) * nt, :] = res_rx[j]
@@ -402,11 +412,9 @@
     for copy in hot_copies:
         copy.start()
     sent += hot_copies
-    hs[-1].wait_recv()
     ps = [None, None]
     for i in (1, 0):
         lo, hi = cuts[i]
-        acc[:, :, lo:hi] += out_part(other, pieces - 1, lo, hi)
         parts_tx[i][...] = acc[:, :, lo:hi].astype(b16)
         ps[i] = [
             remote(
@@ -470,59 +478,62 @@
         load.wait()
 
     tokens = E * drafts
-
-    def expert_part(state, chunk, i):
-        squares, gate, up, logits = state
-        lo, hi = cuts[i]
-        hid = xs[i][chunk].reshape(tokens, hi - lo).astype(f32)
-        cols = pl.ds(pl.multiple_of(chunk * width + lo, 128), hi - lo)
-        scaled = (hid * gains[:, cols]).astype(b16)
-        return (
-            squares + jnp.sum(hid * hid, -1, keepdims=True),
-            gate + jnp.dot(scaled, wg_v[cols, :], preferred_element_type=f32),
-            up + jnp.dot(scaled, wu_v[cols, :], preferred_element_type=f32),
-            logits + lax.dot_general(scaled, rt_v[:, cols], (((1,), (1,)), ((), ())), preferred_element_type=f32),
-        )
-
-    state = (
-        jnp.zeros((tokens, 1), f32),
-        jnp.zeros((tokens, wg_v.shape[1]), f32),
-        jnp.zeros((tokens, wg_v.shape[1]), f32),
-        jnp.zeros((tokens, rt_v.shape[0]), f32),
-    )
-    across = []
-
-    def arrived(state, d):
+    squares[...] = jnp.zeros_like(squares)
+    gate_up[...] = jnp.zeros_like(gate_up)
+    logits[...] = jnp.zeros_like(logits)
+
+    def second_copy(i, hop, d):
+        block = xs[i].at[mine, group_at(hop)] if i else xs[i].at[chunk_at(hop), e]
+        peer = (z_peer if i else e_peer)(d)
+        return remote(block, block, second_sem.at[0, i, hop, d - 1], second_sem.at[1, i, hop, d - 1], peer)
+
+    def across_copy(i, hop):
+        whole = xs[i].at[chunk_at(hop)]
+        return remote(whole, whole, across_sem.at[0, i, hop], across_sem.at[1, i, hop], sibling)
+
+    @pl.loop(0, 2 * R)
+    def _(step):
+        hop = step // 2
+        near_turn = step % 2 == 0
+
+        @pl.when(near_turn)
+        def _():
+            for d in range(1, E):
+                second_copy(0, hop, d).wait_recv()
+            across_copy(0, hop).start()
+
+            @pl.when(hop > 0)
+            def _():
+                for n in range(E):
+                    second_copy(1, n, hop).wait_recv()
+
+            across_copy(1, hop).start()
+
+        @pl.when(jnp.logical_not(near_turn))
+        def _():
+            for i in (0, 1):
+                across_copy(i, hop).wait_recv()
+
+        chunk = lax.rem(r + R - hop, R) * S + lax.rem(s + step, 2)
         for i in (0, 1):
-            across[2 * d + i].wait_recv()
-            state = expert_part(state, lax.rem(r + R - d, R) * S + other, i)
-        return state
-
-    for d in range(R):
-        for i in (0, 1):
-            if i == 0:
-                waits = second[0][d]
-            elif d == 0:
-                waits = []
-            else:
-                waits = [row[d - 1] for row in second[1]]
-            for copy in waits:
-                copy.wait_recv()
-            whole = xs[i].at[chunk_at(d)]
-            copy = remote(whole, whole, across_sem.at[0, i, d], across_sem.at[1, i, d], sibling)
-            copy.start()
-            across.append(copy)
-            state = expert_part(state, chunk_at(d), i)
-        if d:
-            state = arrived(state, d - 1)
-    state = arrived(state, R - 1)
-    sent += across
-    squares, gate, up, logits = state
-    scale = lax.rsqrt(squares / (chunks * width) + 1e-06)
+            lo, hi = cuts[i]
+            hid = xs[i][chunk].reshape(tokens, hi - lo).astype(f32)
+            cols = pl.ds(pl.multiple_of(chunk * width + lo, 128), hi - lo)
+            scaled = (hid * gains[:, cols]).astype(b16)
+            squares[...] += jnp.sum(hid * hid, -1, keepdims=True)
+            gate_up[0] += jnp.dot(scaled, wg_v[cols, :], preferred_element_type=f32)
+            gate_up[1] += jnp.dot(scaled, wu_v[cols, :], preferred_element_type=f32)
+            logits[...] += lax.dot_general(
+                scaled, rt_v[:, cols], (((1,), (1,)), ((), ())), preferred_element_type=f32
+            )
+
+    sent += [across_copy(i, hop) for i in (0, 1) for hop in range(R)]
+    gate, up = gate_up[0], gate_up[1]
+    scale = lax.rsqrt(squares[...] / (chunks * width) + 1e-06)
     experts = rt_v.shape[0]
     for copy in hot_copies:
         copy.wait_recv()
-    chosen = hots[...].reshape(tokens, 128)[:, :experts].astype(f32) * jax.nn.sigmoid(logits * scale)
+    chosen = hots[...].reshape(tokens, 128)[:, :experts].astype(f32) * jax.nn.sigmoid(logits[...] * scale)
     this_expert = lax.broadcasted_iota(jnp.int32, (1, experts), 1) == r
     weight = jnp.sum(jnp.where(this_expert, chosen, 0.0), -1, keepdims=True)
     weight = weight / jnp.sum(chosen, -1, keepdims=True) * 2.5
@@ -660,6 +671,9 @@
         pltpu.VMEM((chunks, nt, width + 128), f32),
         pltpu.VMEM((S * E, nt, width + 128), f32),
         pltpu.VMEM((1, model), f32),
+        pltpu.VMEM((R * drafts, 1), f32),
+        pltpu.VMEM((2, R * drafts, ff), f32),
+        pltpu.VMEM((R * drafts, router.shape[0]), f32),
         pltpu.VMEM((DL // 128, drafts * half_heads, 128), f32),
         pltpu.VMEM((S, pieces, R, drafts, half_heads // pieces * DV), b16),
         pltpu.VMEM((E, drafts, width), f32),

time: 48.3 us -> 50.8 us (1.052)
  Pallas kernels: 46 us -> 48.6 us
    pallas_call x1, Pallas kernels: 46 us -> 48.6 us  [fused(): pl.pallas_call(functools.partial(fused_kernel, dims), out_shape=jax.Shape...]
where the time goes in v5:
time: 50.8 us; the launch traced here: 50.6 us
  Pallas kernels  48.6 us (96%)
  local copies, waits for them, and re-layouts  1.38 us (3%)
  between operations  0.66 us (1%)
    pallas_call x1, Pallas kernels, fused(): pl.pallas_call(functools.partial(fused_kernel, dims), out_shape=jax.Shape...  48.6 us
    unnamed x1, local copies, waits for them, and re-layouts  1.38 us

profile of v5, /device:TPU:0, one launch (start us, length us, event | category | flops | bytes accessed | tf_op | source)
XLA Modules:
  0.0 50.6 jit_solution(16581617190849641869)
XLA Ops:
  0.7 48.6 %shard_map.127 = bf16[2,7168]{1,0:T(2,128)(2,1)} custom-call(bf16[2,7168]{1,0:T(2,128)(2,1)} %residual_ref.1, bf16[16,32,576]{2,1,0:T(8,128)(2,1)} %bitcast.10, bf16[192,576]{1,0:T(8,128)(2,1)} %bitcast.11, s32[2]{0:T(128)} %bitcast.13, s32[1]{0:T(128)S(6)} %copy.15.lengths_ref, bf16[32,512,128]{2,1,0:T(8,128)(2,1)} %value_up_hbm.1, ...), custom_call_target="tpu_custom_call" | custom-call | flops 1174405120 | bytes 22544384 | tf_op jit(solution)/shard_map/pallas_call | solution.py:710
  49.2 1.4 %copy.16 = bf16[2,7168]{1,0:T(2,128)(2,1)} copy(bf16[2,7168]{1,0:T(2,128)(2,1)} %shard_map.127) | data formatting | bytes 57344

commit v6 on v3

--- a/solution.py
+++ b/solution.py
@@ -174,7 +174,8 @@
 
 def column_groups(width):
     cuts = column_cuts(width)
-    return [(lo, min(lo + 256, cuts[0][1])) for lo in range(0, cuts[0][1], 256)] + cuts[1:]
+    first = min(256, cuts[0][1])
+    return [(0, first)] + [(first, cuts[0][1])] * (cuts[0][1] > first) + cuts[1:]
 
 
 def fused_kernel(
@@ -425,9 +426,6 @@
     def chunk_at(d):
         return lax.rem(r + R - d, R) * S + s
 
-    def group_at(d):
-        return lax.rem(e + E - d, E)
-
     first = [None, None]
     for i in (1, 0):
         lo, hi = cuts[i]
@@ -445,27 +443,29 @@
             copy.start()
         sent += first[i]
     second = [[], []]
-    for hop in range(max(R, E)):
-        for i in (1, 0):
-            if hop >= (E if i else R):
-                continue
-            if hop:
-                first[i][hop - 1].wait_recv()
-            block = xs[i].at[mine, group_at(hop)] if i else xs[i].at[chunk_at(hop), e]
-            row = [
-                remote(
-                    block,
-                    block,
-                    second_sem.at[0, i, hop, d - 1],
-                    second_sem.at[1, i, hop, d - 1],
-                    (z_peer if i else e_peer)(d),
-                )
-                for d in range(1, R if i else E)
+    for hop in range(R):
+        if hop:
+            first[0][hop - 1].wait_recv()
+        block = xs[0].at[chunk_at(hop), e]
+        row = [
+            remote(block, block, second_sem.at[0, 0, hop, d - 1], second_sem.at[1, 0, hop, d - 1], e_peer(d))
+            for d in range(1, E)
+        ]
+        for copy in row:
+            copy.start()
+        second[0].append(row)
+        sent += row
+        if hop == 1:
+            for copy in first[1]:
+                copy.wait_recv()
+            whole = xs[1].at[mine]
+            second[1] = [
+                remote(whole, whole, second_sem.at[0, 1, 0, d - 1], second_sem.at[1, 1, 0, d - 1], z_peer(d))
+                for d in range(1, R)
             ]
-            for copy in row:
+            for copy in second[1]:
                 copy.start()
-            second[i].append(row)
-            sent += row
+            sent += second[1]
     for load in loads[3:6]:
         load.wait()
 
@@ -505,7 +505,7 @@
             elif d == 0:
                 waits = []
             else:
-                waits = [row[d - 1] for row in second[1]]
+                waits = [second[1][d - 1]]
             for copy in waits:
                 copy.wait_recv()
             whole = xs[i].at[chunk_at(d)]
@@ -599,7 +599,7 @@
             )
             copy.start()
             end[g].append(copy)
-        sent += [with_core[g]] + mid[g] + end[g]
+        sent += [with_core[g]] + mid[g]
     pick = lax.broadcasted_iota(jnp.int32, (8, tokens), 0) + (mine * E + e) * nt
     pick = (pick == lax.broadcasted_iota(jnp.int32, (8, tokens), 1)).astype(b16)
     own = []
@@ -609,6 +609,14 @@
             for i, (lo, hi) in enumerate(cuts)
         ]
         own.append(jnp.concatenate(sides, axis=1))
+    for copy in sent:
+        copy.wait_send()
+    for c in range(chunks):
+        here = (r == c // S) & (s == c % S) & (e == r)
+
+        @pl.when(jnp.logical_not(here))
+        def _():
+            remote(res_tx.at[c], res_rx.at[slot], res_ssem.at[c], res_rsem.at[slot], (c // S, c % S, r)).wait_send()
     for g in order:
         lo, hi = groups[g]
         routed = mid_sum[g][peers_of(g)[4]]
@@ -619,14 +627,9 @@
             value = own[c][:nt, lo:hi] + routed[c * nt : (c + 1) * nt]
             out_ref[:, c * width + lo : c * width + hi] = value.astype(b16)
 
-    for copy in sent:
-        copy.wait_send()
-    for c in range(chunks):
-        here = (r == c // S) & (s == c % S) & (e == r)
-
-        @pl.when(jnp.logical_not(here))
-        def _():
-            remote(res_tx.at[c], res_rx.at[slot], res_ssem.at[c], res_rsem.at[slot], (c // S, c % S, r)).wait_send()
+    for g in order:
+        for copy in end[g]:
+            copy.wait_send()
 
 
 def fused(
@@ -644,7 +647,7 @@
     ff = w_gate.shape[1]
     per_owner = nt * chunks
     cuts, groups = column_cuts(width), column_groups(width)
-    pieces = 4
+    pieces = 2
     dma = pltpu.SemaphoreType.DMA
     vmem, smem, hbm = (pl.BlockSpec(memory_space=m) for m in (pltpu.VMEM, pltpu.SMEM, pl.ANY))
     scratch = [

time: 48.3 us -> 48.6 us (level)
  no operation moved by 1% of the time
where the time goes in v6:
time: 48.6 us; the launch traced here: 48.4 us
  Pallas kernels  46.4 us (95%)
  local copies, waits for them, and re-layouts  1.38 us (3%)
  between operations  0.66 us (1%)
    pallas_call x1, Pallas kernels, fused(): pl.pallas_call(functools.partial(fused_kernel, dims), out_shape=jax.Shape...  46.4 us
    unnamed x1, local copies, waits for them, and re-layouts  1.38 us

profile of v6, /device:TPU:0, one launch (start us, length us, event | category | flops | bytes accessed | tf_op | source)
XLA Modules:
  0.0 48.4 jit_solution(11308318509952453945)
XLA Ops:
  0.7 46.4 %shard_map.127 = bf16[2,7168]{1,0:T(2,128)(2,1)} custom-call(bf16[2,7168]{1,0:T(2,128)(2,1)} %residual_ref.1, bf16[16,32,576]{2,1,0:T(8,128)(2,1)} %bitcast.10, bf16[192,576]{1,0:T(8,128)(2,1)} %bitcast.11, s32[2]{0:T(128)} %bitcast.13, s32[1]{0:T(128)S(6)} %copy.15.lengths_ref, bf16[32,512,128]{2,1,0:T(8,128)(2,1)} %value_up_hbm.1, ...), custom_call_target="tpu_custom_call" | custom-call | flops 1174405120 | bytes 22544384 | tf_op jit(solution)/shard_map/pallas_call | solution.py:699
  47.0 1.4 %copy.16 = bf16[2,7168]{1,0:T(2,128)(2,1)} copy(bf16[2,7168]{1,0:T(2,128)(2,1)} %shard_map.127) | data formatting | bytes 57344

commit v7 on v3

--- a/solution.py
+++ b/solution.py
@@ -583,6 +583,15 @@
         if n:
             middle(order[n - 1])
     middle(order[-1])
+    pick = lax.broadcasted_iota(jnp.int32, (8, tokens), 0) + (mine * E + e) * nt
+    pick = (pick == lax.broadcasted_iota(jnp.int32, (8, tokens), 1)).astype(b16)
+    own = []
+    for c in range(chunks):
+        sides = [
+            jnp.dot(pick, xs[i][c].reshape(tokens, hi - lo), preferred_element_type=f32)
+            for i, (lo, hi) in enumerate(cuts)
+        ]
+        own.append(jnp.concatenate(sides, axis=1))
     for g in order:
         peer, me, count = peers_of(g)[3:]
         total_g = both[g][:, r] if g == len(groups) - 1 else both[g][e]
@@ -599,16 +608,15 @@
             )
             copy.start()
             end[g].append(copy)
-        sent += [with_core[g]] + mid[g] + end[g]
-    pick = lax.broadcasted_iota(jnp.int32, (8, tokens), 0) + (mine * E + e) * nt
-    pick = (pick == lax.broadcasted_iota(jnp.int32, (8, tokens), 1)).astype(b16)
-    own = []
+        sent += [with_core[g]] + mid[g]
+    for copy in sent:
+        copy.wait_send()
     for c in range(chunks):
-        sides = [
-            jnp.dot(pick, xs[i][c].reshape(tokens, hi - lo), preferred_element_type=f32)
-            for i, (lo, hi) in enumerate(cuts)
-        ]
-        own.append(jnp.concatenate(sides, axis=1))
+        here = (r == c // S) & (s == c % S) & (e == r)
+
+        @pl.when(jnp.logical_not(here))
+        def _():
+            remote(res_tx.at[c], res_rx.at[slot], res_ssem.at[c], res_rsem.at[slot], (c // S, c % S, r)).wait_send()
     for g in order:
         lo, hi = groups[g]
         routed = mid_sum[g][peers_of(g)[4]]
@@ -619,14 +627,9 @@
             value = own[c][:nt, lo:hi] + routed[c * nt : (c + 1) * nt]
             out_ref[:, c * width + lo : c * width + hi] = value.astype(b16)
 
-    for copy in sent:
-        copy.wait_send()
-    for c in range(chunks):
-        here = (r == c // S) & (s == c % S) & (e == r)
-
-        @pl.when(jnp.logical_not(here))
-        def _():
-            remote(res_tx.at[c], res_rx.at[slot], res_ssem.at[c], res_rsem.at[slot], (c // S, c % S, r)).wait_send()
+    for g in order:
+        for copy in end[g]:
+            copy.wait_send()
 
 
 def fused(

time: 48.3 us -> 48.1 us (level)
  no operation moved by 1% of the time
where the time goes in v7:
time: 48.1 us; the launch traced here: 47.9 us
  Pallas kernels  45.9 us (95%)
  local copies, waits for them, and re-layouts  1.38 us (3%)
  between operations  0.66 us (1%)
    pallas_call x1, Pallas kernels, fused(): pl.pallas_call(functools.partial(fused_kernel, dims), out_shape=jax.Shape...  45.9 us
    unnamed x1, local copies, waits for them, and re-layouts  1.38 us

profile of v7, /device:TPU:0, one launch (start us, length us, event | category | flops | bytes accessed | tf_op | source)
XLA Modules:
  0.0 47.9 jit_solution(16415315769825259585)
XLA Ops:
  0.7 45.9 %shard_map.127 = bf16[2,7168]{1,0:T(2,128)(2,1)} custom-call(bf16[2,7168]{1,0:T(2,128)(2,1)} %residual_ref.1, bf16[16,32,576]{2,1,0:T(8,128)(2,1)} %bitcast.10, bf16[192,576]{1,0:T(8,128)(2,1)} %bitcast.11, s32[2]{0:T(128)} %bitcast.13, s32[1]{0:T(128)S(6)} %copy.15.lengths_ref, bf16[32,512,128]{2,1,0:T(8,128)(2,1)} %value_up_hbm.1, ...), custom_call_target="tpu_custom_call" | custom-call | flops 1174405120 | bytes 22544384 | tf_op jit(solution)/shard_map/pallas_call | solution.py:699
  46.5 1.4 %copy.16 = bf16[2,7168]{1,0:T(2,128)(2,1)} copy(bf16[2,7168]{1,0:T(2,128)(2,1)} %shard_map.127) | data formatting | bytes 57344
